TPU v7x, 256 devices: a whole 4x4x8 slice. The times are simulated.
256 devices in a mesh: dp: 2 (over core), expert: 16 (over x, y), tensor: 8 (over z).
Axes of the slice: x: 4, y: 4, z: 8, core: 2. Of those that a mesh axis runs over, the one named last changes fastest.
Arguments:
- tokens: bfloat16 [32768, 1536], P(('dp', 'expert', 'tensor')), may hold values from -6 to 6
- segments: int32 [32, 1024], P(('dp', 'expert')), may hold values from 0 to 18, as said below
- routes: int32 [32768, 8], P(('dp', 'expert', 'tensor')), may hold values from 0 to 31, all different within a row; in each aligned block of 128 rows (0 to 127, 128 to 255, ...) at most 64 rows name the same one
- norm1_gain: float32 [1536], replicated, may hold values from 0.1 to 1.9
- w_query: bfloat16 [1536, 1536], P(None, 'tensor'), may hold values from -0.21875 to 0.21875
- w_key: bfloat16 [1536, 512], P(None, 'tensor'), may hold values from -0.15625 to 0.15625
- w_value: bfloat16 [1536, 512], P(None, 'tensor'), may hold values from -0.15625 to 0.15625
- w_out: bfloat16 [1536, 1536], P('tensor'), may hold values from -0.75 to 0.75
- norm2_gain: float32 [1536], replicated, may hold values from 0.1 to 1.9
- w_router: bfloat16 [1536, 32], replicated, may hold values from -0.078125 to 0.078125
- w_gate: bfloat16 [32, 1536, 512], P('expert', ('dp', 'tensor')), may hold values from -0.15625 to 0.15625
- w_up: bfloat16 [32, 1536, 512], P('expert', ('dp', 'tensor')), may hold values from -0.15625 to 0.15625
- w_down: bfloat16 [32, 512, 1536], P('expert', ('dp', 'tensor')), may hold values from -1 to 1
- cotangent: bfloat16 [32768, 1536], P(('dp', 'expert', 'tensor')), may hold values from -6 to 6
Outputs:
- output: bfloat16 [32768, 1536], P(('dp', 'expert', 'tensor'))
- input_grad: float32 [32768, 1536], P(('dp', 'expert', 'tensor'))
- norm1_gain_grad: float32 [1536], replicated
- w_query_grad: float32 [1536, 1536], P(None, 'tensor')
- w_key_grad: float32 [1536, 512], P(None, 'tensor')
- w_value_grad: float32 [1536, 512], P(None, 'tensor')
- w_out_grad: float32 [1536, 1536], P('tensor')
- norm2_gain_grad: float32 [1536], replicated
- w_router_grad: float32 [1536, 32], replicated
- w_gate_grad: float32 [32, 1536, 512], P('expert', ('dp', 'tensor'))
- w_up_grad: float32 [32, 1536, 512], P('expert', ('dp', 'tensor'))
- w_down_grad: float32 [32, 512, 1536], P('expert', ('dp', 'tensor'))
Inputs may be any that keep to these rules, and one draw needn't show every extreme that they name: `segments`: along a sequence the numbers never fall; 0 marks trailing padding and nothing else, and every sequence ends in at least one padding position; documents are numbered 1, 2, ... in order. Every document but the last of a sequence has 60 to 800 positions; the last may be cut shorter by the padding. In every draw some sequence reaches the largest document number. `routes`: each row names 8 different experts. Within the rows of one device no expert is named by more than 64 rows, and in every draw some device names some expert exactly 64 times.
All inputs are finite; a program needn't handle non-finite values.
Results may differ from a plain program's by a relative error of at most 0.023.
Values may be sent and summed in bfloat16 or wider, within the bound.
No kernel may reach another device: no remote copies, remote signals or barrier semaphores. Data moves between devices by JAX's collectives and lax.ppermute only.
A program may use at most 192 MiB of HBM per device.

v0:
```python
import functools

import jax
import jax.numpy as jnp
import numpy as np
from jax import lax
from jax.experimental import pallas as pl
from jax.experimental.layout import Layout, with_layout_constraint
from jax.experimental.pallas import tpu as pltpu
from jax.sharding import PartitionSpec as P

HEAD_DIM = 64
HALF = HEAD_DIM // 2
TOP = 8
CAP = 64
EXPERTS = 32
HOLDERS = 16
VMEM_BYTES = 57 * 1024 * 1024
LANES = 128

epsilon_norm = 1e-06
rope_theta = 10000.0
masked_score = -1e30
QUERY_ROWS = 512
SCALE = HEAD_DIM ** (-0.5)
f32 = jnp.float32
bf16 = jnp.bfloat16


def rms_inverse(values):
    return lax.rsqrt(jnp.mean(values * values, axis=-1, keepdims=True) + epsilon_norm)


def rms_backward(values, inverse, norm_gain, grad_out):
    scaled = grad_out * norm_gain
    grad_in = inverse * scaled - values * (inverse * inverse * inverse) * jnp.mean(
        scaled * values, axis=-1, keepdims=True
    )
    return (grad_in, grad_out * values * inverse)


def dot32(left, right):
    return jnp.dot(left, right, preferred_element_type=f32)


SIDE = 4
STEPS = (0, 1, -1, 2)


def by_rows(values):
    return with_layout_constraint(values, Layout(major_to_minor=tuple(range(values.ndim))))


def cross(values, stage, step):
    pairs = []
    plane = SIDE * SIDE
    for core in range(2):
        for x in range(SIDE):
            for y in range(SIDE):
                if core == stage:
                    to = x * SIDE + (y + step) % SIDE
                else:
                    to = (x + step) % SIDE * SIDE + y
                pairs.append((core * plane + x * SIDE + y, core * plane + to))
    return lax.ppermute(values, ("dp", "expert"), pairs)


def gather_first(values):
    values = by_rows(values)
    line = jnp.stack([values] + [cross(values, 0, step) for step in STEPS[1:]])
    return by_rows(line)


def gather_second(line):
    return [line] + [cross(line, 1, step) for step in STEPS[1:]]


def scatter_first(parts):
    return [parts[0]] + [
        by_rows(cross(part, 1, -step)) for part, step in zip(parts[1:], STEPS[1:])
    ]


def sum_kernel(*refs):
    arrived, outs = refs[:SIDE], refs[SIDE:]
    total = sum(ref[0].astype(f32) for ref in arrived).astype(bf16)
    for place, out in enumerate(outs):

        @pl.when(pl.program_id(0) == place)
        def _():
            out[...] = total


def sum_first(arrived):
    rows, columns = arrived[0].shape[1:]
    return pl.pallas_call(
        sum_kernel,
        grid=(SIDE,),
        out_shape=[jax.ShapeDtypeStruct((rows, columns), bf16)] * SIDE,
        in_specs=[pl.BlockSpec((1, rows, columns), lambda place: (place, 0, 0))] * SIDE,
        out_specs=[pl.BlockSpec((rows, columns), lambda place: (0, 0))] * SIDE,
        compiler_params=pltpu.CompilerParams(vmem_limit_bytes=24 * 1024 * 1024),
        cost_estimate=pl.CostEstimate(flops=1 << 22, bytes_accessed=8 << 20, transcendentals=0),
    )(*arrived)


def scatter_second(line):
    return [line[0]] + [
        by_rows(cross(part, 0, -step)) for part, step in zip(line[1:], STEPS[1:])
    ]


def ring_sum(values):
    size = lax.axis_size("tensor")
    step = 1
    while step < size:
        pairs = [(i, i ^ step) for i in range(size)]
        values = values + lax.ppermute(values, "tensor", pairs)
        step *= 2
    return values


def together(*values):
    return lax.optimization_barrier(values)


def swap_cores(values):
    return lax.ppermute(values, "dp", [(0, 1), (1, 0)])


def contract(left, right, left_dim, right_dim):
    return lax.dot_general(
        left, right, (((left_dim,), (right_dim,)), ((), ())), preferred_element_type=f32
    )


def allowed(rows, first, wide, col_ref, row_ref):
    query = first + lax.broadcasted_iota(jnp.int32, (rows, wide), 0)
    key = lax.broadcasted_iota(jnp.int32, (rows, wide), 1)
    return (key <= query) & (col_ref[first : first + rows, :] == row_ref[:, :wide])


def probabilities(query, key, mask):
    scores = jnp.where(mask, contract(query, key, 1, 1), masked_score)
    weights = jnp.exp(scores - jnp.max(scores, axis=1, keepdims=True))
    return weights * (1.0 / jnp.sum(weights, axis=1, keepdims=True))


def turn(values, cosine, sine):
    size = values.shape[1]
    first = lax.broadcasted_iota(jnp.int32, values.shape, 1) % HEAD_DIM < HALF
    other = jnp.where(
        first, -pltpu.roll(values, size - HALF, 1), pltpu.roll(values, HALF, 1)
    )
    tables = [jnp.concatenate([table] * (size // LANES), axis=1) for table in (cosine, sine)]
    return values * tables[0] + other * tables[1]


def attention_kernel(
    x_ref, w_ref, col_ref, row_ref, cos_ref, sin_ref, out_ref, turned_ref, qkv_ref
):
    seq_len = out_ref.shape[0]
    tokens = turned_ref.shape[2]
    heads = out_ref.shape[1] // HEAD_DIM
    last = (heads + 1) * HEAD_DIM
    step = QUERY_ROWS
    for first in range(0, seq_len, step):
        at = slice(first, first + step)
        wide = first + step
        blocks = range(first // tokens, wide // tokens)
        rows = jnp.concatenate([x_ref[block, :tokens, :] for block in blocks], axis=0)
        joined = contract(rows, w_ref[...], 1, 1)
        turned_part = turn(joined[:, :last], cos_ref[at, :], sin_ref[at, :])
        qkv_ref[at, :last] = turned_part.astype(bf16)
        qkv_ref[at, last:] = joined[:, last:].astype(bf16)
        mask = allowed(step, first, wide, col_ref, row_ref)
        key = qkv_ref[:wide, heads * HEAD_DIM : last]
        value = qkv_ref[:wide, last:]
        for head in range(heads):
            place = slice(head * HEAD_DIM, (head + 1) * HEAD_DIM)
            query = qkv_ref[at, place] * SCALE
            probs = probabilities(query, key, mask).astype(bf16)
            context = jnp.dot(probs, value, preferred_element_type=f32)
            out_ref[at, place] = context.astype(bf16)
            for block in range(step // tokens):
                turned_ref[first // tokens + block, place, :] = context[
                    block * tokens : (block + 1) * tokens
                ].T.astype(bf16)


def attention_back_kernel(
    qkv_ref, grad_ref, col_ref, row_ref, cos_ref, sin_ref, out_ref, turned_ref, key_sum, value_sum
):
    seq_len = qkv_ref.shape[0]
    heads = grad_ref.shape[1] // HEAD_DIM
    tokens = grad_ref.shape[2]
    last = (heads + 1) * HEAD_DIM
    step = QUERY_ROWS
    for first in reversed(range(0, seq_len, step)):
        at = slice(first, first + step)
        wide = first + step
        mask = allowed(step, first, wide, col_ref, row_ref)
        key = qkv_ref[:wide, heads * HEAD_DIM : last]
        value = qkv_ref[:wide, last:]
        key_grad = jnp.zeros((wide, HEAD_DIM), f32)
        value_grad = jnp.zeros((wide, HEAD_DIM), f32)
        query_grads = []
        for head in range(heads):
            place = slice(head * HEAD_DIM, (head + 1) * HEAD_DIM)
            query = qkv_ref[at, place] * SCALE
            grad = [
                grad_ref[first // tokens + block, place, :].astype(f32).T.astype(bf16)
                for block in range(step // tokens)
            ]
            grad = jnp.concatenate(grad, axis=0)
            probs = probabilities(query, key, mask)
            probs_grad = contract(grad, value, 1, 1)
            row_dot = jnp.sum(probs * probs_grad, axis=1, keepdims=True)
            score_grad = (probs * (probs_grad - row_dot)).astype(bf16)
            query_grads.append(jnp.dot(score_grad, key, preferred_element_type=f32) * SCALE)
            key_grad += contract(score_grad, query, 0, 0)
            value_grad += contract(probs.astype(bf16), grad, 0, 0)
        if wide == seq_len:
            key_sum[...] = key_grad
            value_sum[...] = value_grad
        else:
            key_sum[:wide, :] += key_grad
            value_sum[:wide, :] += value_grad
        both = jnp.concatenate(query_grads + [key_sum[at, :]], axis=1)
        both = turn(both, cos_ref[at, :], -sin_ref[at, :])
        out_ref[at, :last] = both.astype(bf16)
        out_ref[at, last:] = value_sum[at, :].astype(bf16)
        for block in range(step // tokens):
            part = slice(block * tokens, (block + 1) * tokens)
            to = first // tokens + block
            turned_ref[to, :last, :] = both[part].T.astype(bf16)
            turned_ref[to, last:, :] = value_sum[first : first + step, :][part].T.astype(bf16)


def run_attention(gathered, joined_rows, marks, tables):
    planes = gathered.shape[0]
    seq_len = marks[0].shape[0]
    joined_width = joined_rows.shape[0]
    query_width = joined_width - 2 * HEAD_DIM
    vmem = pl.BlockSpec(memory_space=pltpu.VMEM)
    return pl.pallas_call(
        attention_kernel,
        out_shape=(
            jax.ShapeDtypeStruct((seq_len, query_width), bf16),
            jax.ShapeDtypeStruct((planes, query_width, seq_len // planes), bf16),
            jax.ShapeDtypeStruct((seq_len, joined_width), bf16),
        ),
        in_specs=[vmem] * 6,
        out_specs=(vmem,) * 3,
        compiler_params=pltpu.CompilerParams(vmem_limit_bytes=VMEM_BYTES),
        cost_estimate=pl.CostEstimate(
            flops=1 << 28, bytes_accessed=1 << 20, transcendentals=0
        ),
    )(gathered, joined_rows, *marks, *tables)


def run_attention_back(qkv, context_grad, marks, tables):
    seq_len, joined_width = qkv.shape
    planes = context_grad.shape[0]
    vmem = pl.BlockSpec(memory_space=pltpu.VMEM)
    return pl.pallas_call(
        attention_back_kernel,
        out_shape=(
            jax.ShapeDtypeStruct((seq_len, joined_width), bf16),
            jax.ShapeDtypeStruct((planes, joined_width, seq_len // planes), bf16),
        ),
        in_specs=[vmem] * 6,
        out_specs=(vmem, vmem),
        scratch_shapes=[pltpu.VMEM((seq_len, HEAD_DIM), f32)] * 2,
        compiler_params=pltpu.CompilerParams(vmem_limit_bytes=VMEM_BYTES),
        cost_estimate=pl.CostEstimate(
            flops=1 << 28, bytes_accessed=1 << 20, transcendentals=0
        ),
    )(qkv, context_grad, *marks, *tables)


def rope_tables(seq_len):
    frequency = np.float32(rope_theta) ** (np.arange(HALF, dtype=np.float32) * np.float32(-2.0 / HEAD_DIM))
    angles = np.arange(seq_len, dtype=np.float32)[:, None] * frequency.astype(np.float32)[None, :]
    angles = np.tile(angles, (1, LANES // HALF))
    return jnp.asarray(np.cos(angles)), jnp.asarray(np.sin(angles))


def segment_marks(key_seg):
    marks = jnp.where(key_seg == 0, -1 - jnp.arange(key_seg.shape[0], dtype=jnp.int32), key_seg)
    return marks[:, None], marks[None, :]


def expert_kernel(groups, first_ref, *refs):
    rows_refs, cots_refs = refs[:groups], refs[groups : 2 * groups]
    w_ref = refs[2 * groups]
    back_outs = refs[2 * groups + 1 : 3 * groups + 1]
    x_ref, c_ref, gate_ref, up_ref, hid_ref, pick_ref = refs[3 * groups + 1 : 3 * groups + 7]
    down_ref, next_x, next_c, gates_ref = refs[3 * groups + 7 :]
    sources, tokens, _ = rows_refs[0].shape
    width = x_ref.shape[2]
    e = pl.program_id(0)
    expert = first_ref[0] + e
    at = pl.ds(pl.multiple_of(e * CAP, CAP), CAP)
    every = [(group, source) for group in range(groups) for source in range(sources)]

    @pl.when(e == 0)
    def _():
        pair = 2 * CAP
        lane = lax.broadcasted_iota(jnp.int32, (pair, LANES), 1)
        expert_of = expert + lax.broadcasted_iota(jnp.int32, (pair, LANES), 0) // CAP
        own = (lane == expert_of) | (lane == expert_of + EXPERTS)
        row_id = lax.broadcasted_iota(jnp.int32, (EXPERTS, tokens), 0)
        slot = lax.broadcasted_iota(jnp.int32, (pair, tokens), 0)
        place_of = jnp.where(slot < CAP, slot, slot - CAP).astype(f32)
        for order, (group, source) in enumerate(every):
            table = cots_refs[group][source, :EXPERTS, width:].astype(f32)
            ranks = [
                jnp.sum(jnp.where(row_id == expert + i, table, 0.0), axis=0, keepdims=True)
                for i in range(2)
            ]
            pick = (jnp.where(slot < CAP, ranks[0], ranks[1]) == place_of).astype(bf16)
            pick_ref[order] = pick
            rows = jnp.dot(pick, rows_refs[group][source], preferred_element_type=f32)
            cots = jnp.dot(pick, cots_refs[group][source, :, :width], preferred_element_type=f32)
            gate = jnp.sum(jnp.where(own, rows[:, width:], 0.0), axis=1, keepdims=True)
            gate = jnp.broadcast_to(gate, (pair, LANES))
            place = slice(order * CAP, (order + 1) * CAP)
            x_ref[0, place] = rows[:CAP, :width].astype(bf16)
            c_ref[0, place] = cots[:CAP].astype(bf16)
            gates_ref[0, place] = gate[:CAP]
            next_x[place] = rows[CAP:, :width].astype(bf16)
            next_c[place] = cots[CAP:].astype(bf16)
            gates_ref[1, place] = gate[CAP:]

    @pl.when(e == 1)
    def _():
        x_ref[0] = next_x[...]
        c_ref[0] = next_c[...]

    gate = gates_ref[e][:, :1]
    join_chunks(down_ref, w_ref.at[2], HOLDERS)
    x = x_ref[0]
    gate_pre = jnp.dot(x, w_ref[0], preferred_element_type=f32)
    up_pre = jnp.dot(x, w_ref[1], preferred_element_type=f32)
    back = contract(c_ref[0], down_ref[...], 1, 1)
    sig = 1.0 / (1.0 + jnp.exp(-gate_pre))
    silu = gate_pre * sig
    hidden = (silu * up_pre).astype(bf16)
    gate_grad = jnp.sum(back * hidden.astype(f32), axis=1, keepdims=True)
    grad = gate * back
    gate_pre_grad = (grad * up_pre * (sig + silu * (1.0 - sig))).astype(bf16)
    up_pre_grad = (grad * silu).astype(bf16)
    gate_ref[0] = gate_pre_grad
    up_ref[0] = up_pre_grad
    hid_ref[0] = (gate * hidden.astype(f32)).astype(bf16)
    row_grad = contract(gate_pre_grad, w_ref[0], 1, 1) + contract(up_pre_grad, w_ref[1], 1, 1)
    high = gate_grad.astype(bf16).astype(f32)
    lane = lax.broadcasted_iota(jnp.int32, (len(every) * CAP, LANES), 1)
    tail = jnp.where(lane == expert, high, 0.0)
    tail += jnp.where(lane == expert + EXPERTS, gate_grad - high, 0.0)
    for order, (group, source) in enumerate(every):
        place = slice(order * CAP, (order + 1) * CAP)
        back_outs[group][source, at, :width] = row_grad[place].astype(bf16)
        back_outs[group][source, at, width:] = tail[place].astype(bf16)

    @pl.when(e == 1)
    def _():
        for order, (group, source) in enumerate(every):
            back_outs[group][source] = contract(
                pick_ref[order], back_outs[group][source], 0, 0
            ).astype(bf16)


def home_kernel(
    context_ref, w_out_ref, tokens_ref, gain_ref, router_ref, member_ref, mid_ref, inverse_ref, payload_ref, gates_ref
):
    width = tokens_ref.shape[1]
    mid = tokens_ref[...].astype(f32) + contract(context_ref[...], w_out_ref[...], 0, 0)
    inverse = rms_inverse(mid)
    normed = (mid * inverse * gain_ref[...]).astype(bf16)
    mid_ref[...] = mid
    inverse_ref[...] = inverse
    payload_ref[:, :width] = normed
    member = member_ref[...] > 0
    logits = jnp.where(member, contract(normed, router_ref[...], 1, 1), masked_score)
    chosen = jnp.where(member, jnp.exp(logits - jnp.max(logits, axis=1, keepdims=True)), 0.0)
    gates = chosen / jnp.sum(chosen, axis=1, keepdims=True)
    gates_ref[...] = gates
    high = gates.astype(bf16).astype(f32)
    rest = jnp.zeros((gates.shape[0], LANES - 2 * gates.shape[1]), f32)
    payload_ref[:, width:] = jnp.concatenate([high, gates - high, rest], axis=1).astype(bf16)


def run_home(context, w_out, tokens, gain, router, member):
    rows, width = tokens.shape
    vmem = pl.BlockSpec(memory_space=pltpu.VMEM)
    return pl.pallas_call(
        home_kernel,
        out_shape=(
            jax.ShapeDtypeStruct((rows, width), f32),
            jax.ShapeDtypeStruct((rows, 1), f32),
            jax.ShapeDtypeStruct((rows, width + LANES), bf16),
            jax.ShapeDtypeStruct(member.shape, f32),
        ),
        in_specs=[vmem] * 6,
        out_specs=(vmem,) * 4,
        compiler_params=pltpu.CompilerParams(vmem_limit_bytes=24 * 1024 * 1024),
        cost_estimate=pl.CostEstimate(flops=1 << 30, bytes_accessed=8 << 20, transcendentals=0),
    )(context, w_out, tokens, gain, router, member)


def home_back_kernel(*refs):
    parts, refs = refs[:SIDE], refs[SIDE:]
    gates_ref, router_ref, mid_ref, inverse_ref, gain_ref, cot_ref, w_out_ref = refs[:7]
    grad_ref, low_ref, context_ref, logit_ref, norm_ref = refs[7:]
    width = mid_ref.shape[1]
    gates = gates_ref[...]
    experts = gates.shape[1]
    total = sum(ref[...].astype(f32) for ref in parts)
    tail = total[:, width:]
    gate_grad = tail[:, :experts] + tail[:, experts : 2 * experts]
    chosen = gates * (gate_grad - jnp.sum(gates * gate_grad, axis=1, keepdims=True))
    logit_grad = chosen.astype(bf16)
    logit_ref[...] = logit_grad
    normed_grad = total[:, :width] + jnp.dot(
        logit_grad, router_ref[...], preferred_element_type=f32
    )
    mid, inverse = mid_ref[...], inverse_ref[...]
    scaled = normed_grad * gain_ref[...]
    norm_ref[...] = jnp.sum(normed_grad * mid * inverse, axis=0, keepdims=True)
    mean = jnp.mean(scaled * mid, axis=1, keepdims=True)
    grad = cot_ref[...].astype(f32) + inverse * scaled - mid * (inverse * inverse * inverse) * mean
    grad_ref[...] = grad
    low = grad.astype(bf16)
    low_ref[...] = low
    context_ref[...] = contract(w_out_ref[...], low, 1, 1).astype(bf16)


def run_home_back(parts, gates, router, mid, inverse, gain, cotangent, w_out):
    rows, width = mid.shape
    vmem = pl.BlockSpec(memory_space=pltpu.VMEM)
    return pl.pallas_call(
        home_back_kernel,
        out_shape=(
            jax.ShapeDtypeStruct((rows, width), f32),
            jax.ShapeDtypeStruct((rows, width), bf16),
            jax.ShapeDtypeStruct((w_out.shape[0], rows), bf16),
            jax.ShapeDtypeStruct(gates.shape, bf16),
            jax.ShapeDtypeStruct((1, width), f32),
        ),
        in_specs=[vmem] * (SIDE + 7),
        out_specs=(vmem,) * 5,
        compiler_params=pltpu.CompilerParams(vmem_limit_bytes=24 * 1024 * 1024),
        cost_estimate=pl.CostEstimate(flops=1 << 30, bytes_accessed=8 << 20, transcendentals=0),
    )(*parts, gates, router, mid, inverse, gain, cotangent, w_out)


def join_chunks(to_ref, from_ref, holders):
    inner = from_ref.shape[1]
    rows = inner // HOLDERS
    chunks = to_ref.shape[1] // inner
    for holder in range(holders):
        for chunk in range(chunks):
            start = (holder * chunks + chunk) * rows
            to_ref[
                holder * rows : (holder + 1) * rows, chunk * inner : (chunk + 1) * inner
            ] = from_ref[start : start + rows, :]


def run_experts(first, rows, cots, weights):
    groups = len(rows)
    sources, tokens, padded = rows[0].shape
    width = padded - LANES
    inner = weights.shape[2]
    slots = groups * sources * CAP

    def once(columns):
        return pl.BlockSpec(
            (sources, tokens, columns), lambda e: (0, 0, 0), pipeline_mode=pl.Buffered(1)
        )

    def by_expert(*shape):
        return pl.BlockSpec(shape, lambda e: (e, 0, 0))

    acts = jax.ShapeDtypeStruct((2, slots, inner), bf16)
    wide = jax.ShapeDtypeStruct((2, slots, width), bf16)
    outs = pl.pallas_call(
        functools.partial(expert_kernel, groups),
        grid=(2,),
        out_shape=(
            *[jax.ShapeDtypeStruct((sources, tokens, padded), bf16)] * groups,
            wide,
            wide,
            acts,
            acts,
            acts,
            jax.ShapeDtypeStruct((groups * sources, 2 * CAP, tokens), bf16),
        ),
        in_specs=[pl.BlockSpec(memory_space=pltpu.SMEM)]
        + [once(padded)] * (2 * groups)
        + [by_expert(3, width, inner)],
        out_specs=(
            *[once(padded)] * groups,
            by_expert(1, slots, width),
            by_expert(1, slots, width),
            by_expert(1, slots, inner),
            by_expert(1, slots, inner),
            by_expert(1, slots, inner),
            pl.BlockSpec((groups * sources, 2 * CAP, tokens), lambda e: (0, 0, 0)),
        ),
        scratch_shapes=[
            pltpu.VMEM((inner, width), bf16),
            pltpu.VMEM((slots, width), bf16),
            pltpu.VMEM((slots, width), bf16),
            pltpu.VMEM((2, slots, LANES), f32),
        ],
        compiler_params=pltpu.CompilerParams(vmem_limit_bytes=VMEM_BYTES),
        cost_estimate=pl.CostEstimate(
            flops=2 * 2 * 6 * slots * width * inner, bytes_accessed=24 << 20, transcendentals=0
        ),
    )(first, *rows, *cots, weights)
    return outs[:groups], outs[groups:-1], outs[-1]


def mixture_kernel(groups, *refs):
    pick_refs, hid_refs = refs[:groups], refs[groups : 2 * groups]
    w_ref = refs[2 * groups]
    outs, down_ref = refs[2 * groups + 1 : -1], refs[-1]
    e = pl.program_id(0)
    at = pl.ds(pl.multiple_of(e * CAP, CAP), CAP)
    join_chunks(down_ref, w_ref.at[0], HOLDERS)
    sources = [
        (pick_ref, hid_ref, source)
        for pick_ref, hid_ref in zip(pick_refs, hid_refs)
        for source in range(pick_ref.shape[0])
    ]
    to = {}
    for order, (pick_ref, hid_ref, source) in enumerate(sources):
        to[order] = (outs[order // SIDE], order % SIDE, pick_ref, source)
    order = 0
    for pick_ref, hid_ref in zip(pick_refs, hid_refs):
        mixed = jnp.dot(hid_ref[0], down_ref[...], preferred_element_type=f32).astype(bf16)
        for source in range(pick_ref.shape[0]):
            out, place, _, _ = to[order]
            out[place, at] = mixed[source * CAP : (source + 1) * CAP]
            order += 1

    @pl.when(e == 1)
    def _():
        for out, place, pick_ref, source in to.values():
            out[place] = contract(pick_ref[source], out[place], 0, 0).astype(bf16)


def run_mixture(picks, hidden, weights):
    width, inner = weights.shape[1:]
    groups = len(picks)

    def once(shape):
        return pl.BlockSpec(shape, lambda e: (0, 0, 0), pipeline_mode=pl.Buffered(1))

    shapes = [(SIDE, picks[0].shape[2], width)] * SIDE
    return pl.pallas_call(
        functools.partial(mixture_kernel, groups),
        grid=(2,),
        out_shape=[jax.ShapeDtypeStruct(shape, bf16) for shape in shapes],
        in_specs=[once(pick.shape) for pick in picks]
        + [pl.BlockSpec((1,) + hid.shape[1:], lambda e: (e, 0, 0)) for hid in hidden]
        + [pl.BlockSpec((1, width, inner), lambda e: (3 * e + 2, 0, 0))],
        out_specs=[once(shape) for shape in shapes],
        scratch_shapes=[pltpu.VMEM((inner, width), bf16)],
        compiler_params=pltpu.CompilerParams(vmem_limit_bytes=VMEM_BYTES),
        cost_estimate=pl.CostEstimate(flops=1 << 32, bytes_accessed=1 << 20, transcendentals=0),
    )(*picks, *hidden, weights)


def weight_grad_kernel(groups, half_ref, *refs):
    x_refs, c_refs, gate_refs, up_refs, hid_refs = (
        refs[i * groups : (i + 1) * groups] for i in range(5)
    )
    *onto, out_ref = refs[5 * groups :]
    width = x_refs[0].shape[2]
    inner = gate_refs[0].shape[2]
    half = half_ref[0]
    rows = width // 2
    down_rows = inner // HOLDERS
    chunks = width // inner
    cols = pl.ds(pl.multiple_of(half * rows, LANES), rows)
    down_cols = pl.ds(pl.multiple_of(half * (inner // 2), LANES), inner // 2)
    gate = jnp.zeros((rows, inner), f32)
    up = jnp.zeros((rows, inner), f32)
    down = jnp.zeros((inner // 2, width), f32)
    for i in range(groups):
        x = x_refs[i][0, :, cols]
        gate += contract(x, gate_refs[i][0], 0, 0)
        up += contract(x, up_refs[i][0], 0, 0)

    def put(place, at, values):
        if onto:
            values = values + onto[0][place, at, :].astype(f32)
        out_ref[place, at, :] = values.astype(bf16)

    put(0, slice(0, rows), gate)
    put(1, slice(0, rows), up)
    for i in range(groups):
        down += contract(hid_refs[i][0, :, down_cols], c_refs[i][0], 0, 0)
    for holder in range(HOLDERS // 2):
        for chunk in range(chunks):
            start = (holder * chunks + chunk) * down_rows
            put(
                2,
                slice(start, start + down_rows),
                down[
                    holder * down_rows : (holder + 1) * down_rows,
                    chunk * inner : (chunk + 1) * inner,
                ],
            )


def run_weight_grads(half, saved, *onto):
    x, c, gate, up, hid = zip(*saved)
    width = x[0].shape[2]
    inner = gate[0].shape[2]
    operands = (*x, *c, *gate, *up, *hid)
    out_spec = pl.BlockSpec((3, width // 2, inner), lambda e: (e, 0, 0))
    return pl.pallas_call(
        functools.partial(weight_grad_kernel, len(saved)),
        grid=(2,),
        out_shape=jax.ShapeDtypeStruct((6, width // 2, inner), bf16),
        in_specs=[pl.BlockSpec(memory_space=pltpu.SMEM)]
        + [pl.BlockSpec((1,) + v.shape[1:], lambda e: (e, 0, 0)) for v in operands]
        + [out_spec] * len(onto),
        out_specs=out_spec,
        compiler_params=pltpu.CompilerParams(vmem_limit_bytes=VMEM_BYTES),
        cost_estimate=pl.CostEstimate(flops=1 << 28, bytes_accessed=1 << 20, transcendentals=0),
    )(half, *operands, *onto)


def joined_kernel(
    x_ref, grad_ref, w_ref, normed_ref, logit_ref, norm_ref, gain_ref, out_ref, shared_ref
):
    planes = x_ref.shape[0]
    tokens = grad_ref.shape[0] // planes
    experts = logit_ref.shape[1]
    step = x_ref.shape[2] // 2
    for first in range(0, x_ref.shape[2], step):
        at = slice(first, first + step)
        rows = jnp.concatenate([x_ref[plane, :tokens, at] for plane in range(planes)], axis=0)
        joined = contract(grad_ref[...], rows, 0, 0)
        out_ref[:, at] = joined.astype(bf16)
        norm1 = jnp.sum(joined * w_ref[:, at].astype(f32), axis=0, keepdims=True) / gain_ref[:, at]
        shared_ref[:experts, at] = contract(logit_ref[...], normed_ref[:, at], 0, 0).astype(bf16)
        shared_ref[experts : experts + 1, at] = norm_ref[:, at].astype(bf16)
        shared_ref[experts + 1 : experts + 2, at] = norm1.astype(bf16)


def run_joined(gathered, joined_grad, joined_rows, normed_two, logits, norm_terms, gain):
    vmem = pl.BlockSpec(memory_space=pltpu.VMEM)
    width = gathered.shape[2]
    return pl.pallas_call(
        joined_kernel,
        out_shape=(
            jax.ShapeDtypeStruct((joined_grad.shape[1], width), bf16),
            jax.ShapeDtypeStruct((logits.shape[1] + 2, width), bf16),
        ),
        in_specs=[vmem] * 7,
        out_specs=(vmem, vmem),
        compiler_params=pltpu.CompilerParams(vmem_limit_bytes=VMEM_BYTES),
        cost_estimate=pl.CostEstimate(flops=1 << 20, bytes_accessed=1 << 16, transcendentals=0),
    )(gathered, joined_grad, joined_rows, normed_two, logits, norm_terms, gain)


def out_kernel(all_ref, context_ref, out_ref):
    out_ref[...] = contract(context_ref[...], all_ref[...], 0, 0).astype(bf16)


def run_out(attention_all, context):
    width = attention_all.shape[1]
    rows, columns = context.shape
    step = width // 4
    return pl.pallas_call(
        out_kernel,
        grid=(4,),
        out_shape=jax.ShapeDtypeStruct((columns, width), bf16),
        in_specs=[
            pl.BlockSpec((rows, step), lambda i: (0, i)),
            pl.BlockSpec((rows, columns), lambda i: (0, 0)),
        ],
        out_specs=pl.BlockSpec((columns, step), lambda i: (0, i)),
        compiler_params=pltpu.CompilerParams(vmem_limit_bytes=VMEM_BYTES),
        cost_estimate=pl.CostEstimate(flops=1 << 20, bytes_accessed=1 << 16, transcendentals=0),
    )(attention_all, context)


def local(
    tokens,
    segments,
    routes,
    norm1_gain,
    w_query,
    w_key,
    w_value,
    w_out,
    norm2_gain,
    w_router,
    w_gate,
    w_up,
    w_down,
    cotangent,
):
    tok_rows, width = tokens.shape
    seq_len = segments.shape[1]
    query_width = w_query.shape[1]
    kv_width = w_key.shape[1]
    joined_width = query_width + 2 * kv_width
    local_experts = w_gate.shape[0]
    experts = w_router.shape[1]
    owners = lax.axis_size("expert")
    planes = lax.axis_size("tensor")
    owner = lax.axis_index("expert")
    first_expert = owner * local_experts
    key_seg = segments[0]
    hidden_width = w_gate.shape[2]

    token_f32 = tokens.astype(f32)
    inverse_one = rms_inverse(token_f32)
    normed_low = (token_f32 * inverse_one * norm1_gain).astype(bf16)
    joined_rows = by_rows(jnp.concatenate([w_query.T, w_key.T, w_value.T], axis=0))
    core = lax.axis_index("dp")

    def half_of(rows):
        count = rows.shape[0] // 2
        return lax.dynamic_slice_in_dim(rows, core * count, count, 0)

    place = jnp.where(core == 0, owner % SIDE, owner // SIDE)
    quarter = w_out.shape[0] // SIDE
    w_out_part = lax.dynamic_slice_in_dim(w_out, place * quarter, quarter, 0)
    gathered = lax.all_gather(
        by_rows(jnp.concatenate([normed_low, w_out_part], axis=0)), "tensor", axis=0
    )

    expert_ids = jnp.arange(experts, dtype=jnp.int32)
    onehot = (routes[:, :, None] == expert_ids[None, None, :]).astype(f32)
    member = jnp.sum(onehot, axis=1)
    lower = (jnp.arange(tok_rows)[:, None] <= jnp.arange(tok_rows)[None, :]).astype(bf16)
    rank = jnp.einsum("te,tu->eu", member.astype(bf16), lower, preferred_element_type=f32)
    rank = jnp.where(member.T > 0, rank - 1.0, -1.0).astype(bf16)
    extra = jnp.pad(rank, ((0, tok_rows - experts), (0, LANES - tok_rows)))
    cot_payload = jnp.concatenate([cotangent, extra], axis=1)

    chunks = width // hidden_width
    down_rows = w_down.shape[1]
    part_rows = w_gate.shape[1]
    down_parts = w_down.reshape(local_experts, down_rows, chunks, hidden_width)
    down_parts = down_parts.transpose(0, 2, 1, 3).reshape(local_experts, part_rows, hidden_width)
    weights = jnp.stack([w_gate, w_up, down_parts], axis=1)
    weights = weights.reshape(3 * local_experts, part_rows, hidden_width)
    tables = rope_tables(seq_len)
    marks = segment_marks(key_seg)
    cot_parts = gather_second(gather_first(cot_payload))
    joined_half = by_rows(half_of(joined_rows))
    gathered, weights, joined_rows, joined_half, member, col, row, *cot_parts = together(
        gathered, weights, joined_rows, joined_half, by_rows(member), *marks, *cot_parts
    )
    marks = col, row
    weights_all = lax.all_gather(weights, ("dp", "tensor"), axis=1, tiled=True)
    quarters = by_rows(gathered[:, tok_rows:])
    quarters = [quarters] + [by_rows(cross(quarters, 0, step)) for step in STEPS[1:]]
    context, context_blocks, qkv = run_attention(gathered, joined_rows, marks, tables)
    context_home = lax.all_to_all(context_blocks, "tensor", split_axis=0, concat_axis=0)
    w_out_all = jnp.zeros((planes, SIDE * quarter, width), bf16)
    for step, part in zip(STEPS, quarters):
        start = (place - step) % SIDE * quarter
        w_out_all = lax.dynamic_update_slice(w_out_all, part, (0, start, 0))
    w_out_all = by_rows(w_out_all.reshape(-1, width))
    context_home, w_out_all, joined_half = together(context_home, w_out_all, joined_half)
    half_joined = lax.all_gather(joined_half, "tensor", axis=0)
    router = by_rows(w_router.T)
    mid, inverse_two, payload, gates = run_home(
        context_home.reshape(planes * query_width, tok_rows),
        w_out_all,
        tokens,
        norm2_gain[None],
        router,
        member,
    )
    line = gather_first(payload)
    before, behind = (cross(line, 1, step) for step in STEPS[1:3])

    first_expert = first_expert.astype(jnp.int32).reshape(1)
    def compute(rows, cots):
        return run_experts(first_expert, rows, cots, weights_all)

    own = compute([line], cot_parts[:1])
    line, before, behind, *own_saved = together(line, before, behind, *own[1])
    far = cross(line, 1, STEPS[3])
    near = compute([before, behind], cot_parts[1:3])
    far, *near_saved = together(far, *near[1])
    last = compute([far], cot_parts[3:])
    done = [(*own[0], *near[0], *last[0]), (own_saved, near_saved, last[1])]
    back_line = scatter_first(done[0])
    mix_parts = run_mixture(
        [own[2], near[2], last[2]], [own_saved[4], near_saved[4], last[1][4]], weights_all
    )
    given = run_weight_grads((1 - core).astype(jnp.int32).reshape(1), done[1])
    n_line = len(back_line)
    *both, given, half_joined = together(*back_line, *mix_parts, given, half_joined)
    back_line, mix_parts = sum_first(both[:n_line]), both[n_line:]
    back_home = scatter_second(back_line)
    back_home[1], received = together(back_home[1], swap_cores(given))

    mid_grad, attention_low, context_grad, logit_grad, norm2_part = run_home_back(
        back_home, gates, router, mid, inverse_two, norm2_gain[None], cotangent, w_out_all
    )
    received, *mix_parts, context_grad, logit_grad = together(
        received, *mix_parts, context_grad, logit_grad
    )
    mix_arrived = scatter_first(mix_parts)
    kept = run_weight_grads(core.astype(jnp.int32).reshape(1), done[1], received)
    context_grad = lax.all_to_all(
        context_grad.reshape(planes, query_width, tok_rows), "tensor", split_axis=0, concat_axis=0
    )
    context_grad, kept = together(context_grad, kept)
    joined_grad, joined_blocks = run_attention_back(qkv, context_grad, marks, tables)
    joined_home = lax.all_to_all(joined_blocks, "tensor", split_axis=0, concat_axis=0)
    attention_all = lax.all_gather(attention_low, "tensor", axis=0, tiled=True)
    joined_part, shared = run_joined(
        gathered, joined_grad, joined_rows, payload, logit_grad, norm2_part, norm1_gain[None]
    )
    sides = jnp.concatenate([joined_part, run_out(attention_all, context)], axis=0)

    share = sides.shape[0] // (2 * owners)
    shared_shape = shared.shape
    shared_rows = shared.size // LANES
    shared = shared.reshape(shared_rows, LANES)
    shared = jnp.pad(shared, ((0, 2 * owners * share - shared_rows), (0, 0)))
    blocks = jnp.concatenate(
        [sides.reshape(2, owners, share, width), shared.reshape(2, owners, share, LANES)], axis=3
    )
    def of_core(which):
        return lax.dynamic_index_in_dim(blocks, which, 0, keepdims=False)

    blocks, theirs, joined_home, kept, *mix_arrived = together(
        blocks, swap_cores(of_core(1 - core)), joined_home, kept, *mix_arrived
    )
    weight_sum = lax.psum_scatter(kept, "tensor", scatter_dimension=1, tiled=True)

    part = of_core(core).astype(f32) + theirs.astype(f32)
    arrived = lax.all_to_all(part.astype(bf16), "expert", split_axis=0, concat_axis=0)

    def rows_of(which):
        count = joined_width // 2
        rows = lax.dynamic_slice_in_dim(joined_home, which * count, count, 1)
        return rows.reshape(-1, tok_rows)

    normed_one_grad = contract(rows_of(core), half_joined.reshape(-1, width), 0, 0)
    normed_one_grad += contract(
        rows_of(1 - core), swap_cores(half_joined).reshape(-1, width), 0, 0
    )
    arrived, normed_one_grad, *mix_line = together(
        arrived, normed_one_grad, *sum_first(mix_arrived)
    )
    total = jnp.sum(arrived.astype(f32), axis=0)
    total = jnp.concatenate([total[:, :width], ring_sum(total[:, width:])], axis=1).astype(bf16)
    spread = lax.all_to_all(
        jnp.broadcast_to(total[None], arrived.shape), "expert", split_axis=0, concat_axis=0
    )
    mixture = sum(part.astype(f32) for part in scatter_second(mix_line))
    spread, mixture = together(by_rows(spread), mixture)
    output = (mid + mixture).astype(bf16)
    spread, weight_sum = together(spread, weight_sum)
    other = swap_cores(spread)
    first, second = jnp.where(core == 0, spread, other), jnp.where(core == 0, other, spread)
    shared = jnp.concatenate([first, second], axis=0)[:, :, width:].reshape(-1, LANES)
    shared = shared[:shared_rows].astype(f32).reshape(shared_shape)
    first = first[:, :, :width].reshape(-1, width)
    second = second[:, :, :width].reshape(-1, width)
    query_sum = first[:query_width].astype(f32).T
    key_sum = first[query_width:].astype(f32).T
    value_sum = second[:kv_width].astype(f32).T
    out_sum = second[kv_width:].astype(f32)
    weight_sum = weight_sum.reshape(local_experts, 3, part_rows, hidden_width)
    w_gate_grad = weight_sum[:, 0].astype(f32)
    w_up_grad = weight_sum[:, 1].astype(f32)
    w_down_grad = weight_sum[:, 2].reshape(local_experts, chunks, down_rows, hidden_width)
    w_down_grad = w_down_grad.transpose(0, 2, 1, 3).reshape(local_experts, down_rows, width)
    w_down_grad = w_down_grad.astype(f32)
    input_part, _ = rms_backward(token_f32, inverse_one, norm1_gain, normed_one_grad)
    input_grad = mid_grad + input_part
    return (
        output,
        input_grad,
        shared[experts + 1],
        query_sum,
        key_sum,
        value_sum,
        out_sum,
        shared[experts],
        shared[:experts].T,
        w_gate_grad,
        w_up_grad,
        w_down_grad,
    )


def solution(mesh):
    rows = P(("dp", "expert", "tensor"), None)
    columns = P(None, "tensor")
    experts = P("expert", ("dp", "tensor"), None)
    return jax.shard_map(
        local,
        mesh=mesh,
        in_specs=(
            rows,
            P(("dp", "expert"), None),
            rows,
            P(),
            columns,
            columns,
            columns,
            P("tensor", None),
            P(),
            P(),
            experts,
            experts,
            experts,
            rows,
        ),
        out_specs=(
            rows,
            rows,
            P(),
            columns,
            columns,
            columns,
            P("tensor", None),
            P(),
            P(),
            experts,
            experts,
            experts,
        ),
        check_vma=False,
    )
```

profile of v0, /device:TPU:1, one launch (start us, length us, event | category | flops | bytes accessed | tf_op | source)
XLA Modules:
  0.0 396.1 jit_solution(10848400541339062680)
XLA Ops:
  16.0 4.3 %collective-permute-done.2 = bf16[128,1664]{1,0:T(8,128)(2,1)S(1)} collective-permute-done((bf16[128,1664]{1,0:T(8,128)(2,1)S(1)}, bf16[128,1664]{1,0:T(8,128)(2,1)S(1)}, u32[]{:S(2)}, u32[]{:S(2)}) %collective-permute-start.2) | collective-permute-done | bytes 426016 | tf_op jit(solution)/shard_map/ppermute | solution.py:65
  20.4 4.9 %collective-permute-done.1 = bf16[128,1664]{1,0:T(8,128)(2,1)S(1)} collective-permute-done((bf16[128,1664]{1,0:T(8,128)(2,1)S(1)}, bf16[128,1664]{1,0:T(8,128)(2,1)S(1)}, u32[]{:S(2)}, u32[]{:S(2)}) %collective-permute-start.1) | collective-permute-done | bytes 426016 | tf_op jit(solution)/shard_map/ppermute | solution.py:65
  36.1 13.3 %collective-permute-done.3.refs_2_ = bf16[4,128,1664]{2,1,0:T(8,128)(2,1)} collective-permute-done((bf16[4,128,1664]{2,1,0:T(8,128)(2,1)}, bf16[4,128,1664]{2,1,0:T(8,128)(2,1)}, u32[]{:S(2)}, u32[]{:S(2)}) %collective-permute-start.3) | collective-permute-done | bytes 1703968 | tf_op jit(solution)/shard_map/ppermute | solution.py:65
  49.4 19.4 %collective-permute-done.5.refs_1_ = bf16[4,128,1664]{2,1,0:T(8,128)(2,1)} collective-permute-done((bf16[4,128,1664]{2,1,0:T(8,128)(2,1)}, bf16[4,128,1664]{2,1,0:T(8,128)(2,1)}, u32[]{:S(2)}, u32[]{:S(2)}) %collective-permute-start.5) | collective-permute-done | bytes 1703968 | tf_op jit(solution)/shard_map/ppermute | solution.py:65
  80.4 10.5 %shard_map.247 = (bf16[1024,192]{1,0:T(8,128)(2,1)}, bf16[8,192,128]{2,1,0:T(8,128)(2,1)}, bf16[1024,320]{1,0:T(8,128)(2,1)}) custom-call(bf16[8,176,1536]{2,1,0:T(8,128)(2,1)} %bitcast.96, bf16[320,1536]{1,0:T(8,128)(2,1)} %copy-done.16, s32[1024,1]{1,0:T(8,128)} %compare_select_fusion.col_ref, s32[1,1024]{1,0:T(1,128)} %compare_select_fusion.1.row_ref, ...), custom_call_target="tpu_custom_call" | custom-call | flops 268435456 | bytes 1048576 | tf_op jit(solution)/shard_map/pallas_call | solution.py:246
  90.9 6.0 %all-to-all-start = ((bf16[8,192,128]{2,1,0:T(8,128)(2,1)}), bf16[8,192,128]{2,1,0:T(8,128)(2,1)S(1)}, u32[]{:S(2)}, u32[]{:S(2)}) async-start(bf16[8,192,128]{2,1,0:T(8,128)(2,1)} %get-tuple-element.133), calls=%async_computation | async-start | bytes 786432 | tf_op jit(solution)/shard_map/all_to_all | solution.py:770
  99.4 5.6 %collective-permute-done.7 = bf16[8,48,1536]{2,1,0:T(8,128)(2,1)} collective-permute-done((bf16[8,48,1536]{2,1,0:T(8,128)(2,1)}, bf16[8,48,1536]{2,1,0:T(8,128)(2,1)}, u32[]{:S(2)}, u32[]{:S(2)}) %collective-permute-start.7) | collective-permute-done | bytes 1179680 | tf_op jit(solution)/shard_map/ppermute | solution.py:65
  108.4 6.1 %all-to-all-done = bf16[8,192,128]{2,1,0:T(8,128)(2,1)S(1)} async-done(((bf16[8,192,128]{2,1,0:T(8,128)(2,1)}), bf16[8,192,128]{2,1,0:T(8,128)(2,1)S(1)}, u32[]{:S(2)}, u32[]{:S(2)}) %all-to-all-start) | async-done | bytes 393248 | tf_op jit(solution)/shard_map/all_to_all | solution.py:770
  122.5 4.7 %collective-permute-done.11 = bf16[128,1664]{1,0:T(8,128)(2,1)S(1)} collective-permute-done((bf16[128,1664]{1,0:T(8,128)(2,1)S(1)}, bf16[128,1664]{1,0:T(8,128)(2,1)S(1)}, u32[]{:S(2)}, u32[]{:S(2)}) %collective-permute-start.11) | collective-permute-done | bytes 426016 | tf_op jit(solution)/shard_map/ppermute | solution.py:65
  136.5 5.7 %all-gather.7.cloned.1.call-done.refs_2_.refs_4_.refs_6_ = bf16[6,1536,512]{2,1,0:T(8,128)(2,1)} async-done(((bf16[6,96,512]{2,1,0:T(8,128)(2,1)}), bf16[6,1536,512]{2,1,0:T(8,128)(2,1)}) %all-gather.7.cloned.1.call-update) | async-done | bytes 9437200 | tf_op jit(solution)/shard_map/all_gather | solution.py:766
  142.2 11.9 %shard_map.249 = (bf16[4,128,1664]{2,1,0:T(8,128)(2,1)}, bf16[2,256,1536]{2,1,0:T(8,128)(2,1)}, bf16[2,256,1536]{2,1,0:T(8,128)(2,1)}, bf16[2,256,512]{2,1,0:T(8...) custom-call(s32[1]{0:T(128)} %bitcast.18.first_ref, ...), custom_call_target="tpu_custom_call" | custom-call | flops 4831838208 | bytes 25165824 | tf_op jit(solution)/shard_map/pallas_call | solution.py:488
  158.3 20.1 %shard_map.250 = (bf16[4,128,1664]{2,1,0:T(8,128)(2,1)}, bf16[4,128,1664]{2,1,0:T(8,128)(2,1)}, bf16[2,512,1536]{2,1,0:T(8,128)(2,1)}, bf16[2,512,1536]{2,1,0:T(...) custom-call(s32[1]{0:T(128)} %bitcast.18.first_ref, ...), custom_call_target="tpu_custom_call" | custom-call | flops 9663676416 | bytes 25165824 | tf_op jit(solution)/shard_map/pallas_call | solution.py:488
  181.7 12.0 %shard_map.251 = (bf16[4,128,1664]{2,1,0:T(8,128)(2,1)}, bf16[2,256,1536]{2,1,0:T(8,128)(2,1)}, bf16[2,256,1536]{2,1,0:T(8,128)(2,1)}, bf16[2,256,512]{2,1,0:T(8...) custom-call(s32[1]{0:T(128)} %bitcast.18.first_ref, ...), custom_call_target="tpu_custom_call" | custom-call | flops 4831838208 | bytes 25165824 | tf_op jit(solution)/shard_map/pallas_call | solution.py:488
  195.1 10.5 %shard_map.253 = bf16[6,768,512]{2,1,0:T(8,128)(2,1)} custom-call(s32[1]{0:T(128)} %bitcast.23.half_ref, bf16[2,256,1536]{2,1,0:T(8,128)(2,1)} %get-tuple-element.174.refs_0_, bf16[2,512,1536]{2,1,0:T(8,128)(2,1)} %get-tuple-element.175.refs_1_, bf16[2,256,1536]{2,1,0:T(8,128)(2,1)} %get-tuple-element.176.refs_2_, ...), custom_call_target="tpu_custom_call" | custom-call | flops 268435456 | bytes 1048576 | tf_op jit(solution)/shard_map/pallas_call | solution.py:626
  205.6 10.3 %shard_map.252 = (bf16[4,128,1536]{2,1,0:T(8,128)(2,1)}, bf16[4,128,1536]{2,1,0:T(8,128)(2,1)}, bf16[4,128,1536]{2,1,0:T(8,128)(2,1)}, bf16[4,128,1536]{2,1,0:T(8,128)(2,1)}) custom-call(bf16[4,128,128]{2,1,0:T(8,128)(2,1)} %get-tuple-element.164.refs_0_, bf16[8,128,128]{2,1,0:T(8,128)(2,1)} %get-tuple-element.165.refs_1_, ...), custom_call_target="tpu_custom_call" | custom-call | flops 4294967296 | bytes 1048576 | tf_op jit(solution)/shard_map/pallas_call | solution.py:563
  221.2 7.3 %collective-permute-start.19 = (bf16[6,768,512]{2,1,0:T(8,128)(2,1)}, bf16[6,768,512]{2,1,0:T(8,128)(2,1)S(1)}, u32[]{:S(2)}, u32[]{:S(2)}) collective-permute-start(bf16[6,768,512]{2,1,0:T(8,128)(2,1)} %shard_map.253), channel_id=1, source_target_pairs={{0,128},{128,0},{1,129},{129,1},{2,130},{130,2},{3,131},{131,3},{4... | collective-permute-start | bytes 14155784 | tf_op jit(solution)/shard_map/ppermute | solution.py:128
  234.2 5.5 %collective-permute-done.18.refs_1_ = bf16[128,1664]{1,0:T(8,128)(2,1)S(1)} collective-permute-done((bf16[128,1664]{1,0:T(8,128)(2,1)S(1)}, bf16[128,1664]{1,0:T(8,128)(2,1)S(1)}, u32[]{:S(2)}, u32[]{:S(2)}) %collective-permute-start.18) | collective-permute-done | bytes 426016 | tf_op jit(solution)/shard_map/ppermute | solution.py:65
  239.7 5.9 %collective-permute-done.20.refs_2_ = bf16[128,1664]{1,0:T(8,128)(2,1)S(1)} collective-permute-done((bf16[128,1664]{1,0:T(8,128)(2,1)S(1)}, bf16[128,1664]{1,0:T(8,128)(2,1)S(1)}, u32[]{:S(2)}, u32[]{:S(2)}) %collective-permute-start.20) | collective-permute-done | bytes 426016 | tf_op jit(solution)/shard_map/ppermute | solution.py:65
  245.6 5.3 %shard_map.255 = (f32[128,1536]{1,0:T(8,128)S(1)}, bf16[128,1536]{1,0:T(8,128)(2,1)}, bf16[1536,128]{1,0:T(8,128)(2,1)}, bf16[128,32]{1,0:T(8,128)(2,1)S(1)}, f32[1,1536]{1,0:T(1,128)S(1)}) custom-call(bf16[128,1664]{1,0:T(8,128)(2,1)S(1)} %get-tuple-element.198.refs_0_, bf16[128,1664]{1,0:T(8,128)(2,1)S(1)} %collective-permute-done.18.refs_1_, ...), custom_call_target="tpu_custom_call" | custom-call | flops 1073741824 | bytes 8388608 | tf_op jit(solution)/shard_map/pallas_call | solution.py:443
  260.0 12.3 %shard_map.256 = bf16[6,768,512]{2,1,0:T(8,128)(2,1)} custom-call(s32[1]{0:T(128)} %bitcast.26.half_ref, bf16[2,256,1536]{2,1,0:T(8,128)(2,1)} %get-tuple-element.174.refs_0_, bf16[2,512,1536]{2,1,0:T(8,128)(2,1)} %get-tuple-element.175.refs_1_, bf16[2,256,1536]{2,1,0:T(8,128)(2,1)} %get-tuple-element.176.refs_2_, ...), custom_call_target="tpu_custom_call" | custom-call | flops 268435456 | bytes 1048576 | tf_op jit(solution)/shard_map/pallas_call | solution.py:626
  273.1 13.5 %shard_map.257 = (bf16[1024,320]{1,0:T(8,128)(2,1)}, bf16[8,320,128]{2,1,0:T(8,128)(2,1)}) custom-call(bf16[1024,320]{1,0:T(8,128)(2,1)} %get-tuple-element.139.qkv_ref, bf16[8,192,128]{2,1,0:T(8,128)(2,1)} %copy-done.21, s32[1024,1]{1,0:T(8,128)} %compare_select_fusion.col_ref, s32[1,1024]{1,0:T(1,128)} %compare_select_fusion.1.row_ref, ...), custom_call_target="tpu_custom_call" | custom-call | flops 268435456 | bytes 1048576 | tf_op jit(solution)/shard_map/pallas_call | solution.py:266
  286.6 5.2 %shard_map.258 = (bf16[320,1536]{1,0:T(8,128)(2,1)}, bf16[34,1536]{1,0:T(8,128)(2,1)}) custom-call(bf16[8,176,1536]{2,1,0:T(8,128)(2,1)} %bitcast.97, bf16[1024,320]{1,0:T(8,128)(2,1)} %get-tuple-element.209.grad_ref, bf16[320,1536]{1,0:T(8,128)(2,1)} %copy-done.16, bf16[128,1664]{1,0:T(8,128)(2,1)} %copy-done.3, bf16[128,32]{1,0:T(8,128)(2,1)} %copy-done.12, ...), custom_call_target="tpu_custom_call" | custom-call | flops 1048576 | bytes 65536 | tf_op jit(solution)/shard_map/pallas_call | solution.py:660
  292.8 6.7 %all-to-all-start.2 = ((bf16[8,320,128]{2,1,0:T(8,128)(2,1)}), bf16[8,320,128]{2,1,0:T(8,128)(2,1)S(1)}, u32[]{:S(2)}, u32[]{:S(2)}) async-start(bf16[8,320,128]{2,1,0:T(8,128)(2,1)} %get-tuple-element.216), calls=%async_computation.2 | async-start | bytes 1310720 | tf_op jit(solution)/shard_map/all_to_all | solution.py:825
  299.6 4.9 %shard_map.259 = bf16[192,1536]{1,0:T(8,128)(2,1)} custom-call(bf16[1024,1536]{1,0:T(8,128)(2,1)} %all-gather.9.cloned.1.call-done.all_ref, bf16[1024,192]{1,0:T(8,128)(2,1)} %get-tuple-element.214.context_ref), custom_call_target="tpu_custom_call" | custom-call | flops 1048576 | bytes 65536 | tf_op jit(solution)/shard_map/pallas_call | solution.py:681
  310.3 7.7 %all-to-all-done.2 = bf16[8,320,128]{2,1,0:T(8,128)(2,1)S(1)} async-done(((bf16[8,320,128]{2,1,0:T(8,128)(2,1)}), bf16[8,320,128]{2,1,0:T(8,128)(2,1)S(1)}, u32[]{:S(2)}, u32[]{:S(2)}) %all-to-all-start.2) | async-done | bytes 655392 | tf_op jit(solution)/shard_map/all_to_all | solution.py:825
  324.3 4.4 %all-to-all-start.3 = ((bf16[16,16,1664]{2,1,0:T(8,128)(2,1)}), bf16[16,16,1664]{2,1,0:T(8,128)(2,1)}, u32[]{:S(2)}, u32[]{:S(2)}) async-start(bf16[16,16,1664]{2,1,0:T(8,128)(2,1)} %fusion.1), calls=%async_computation.3 | async-start | bytes 1703936 | tf_op jit(solution)/shard_map/all_to_all | solution.py:849
  338.0 5.0 %all-to-all-done.3 = bf16[16,16,1664]{2,1,0:T(8,128)(2,1)} async-done(((bf16[16,16,1664]{2,1,0:T(8,128)(2,1)}), bf16[16,16,1664]{2,1,0:T(8,128)(2,1)}, u32[]{:S(2)}, u32[]{:S(2)}) %all-to-all-start.3) | async-done | bytes 852000 | tf_op jit(solution)/shard_map/all_to_all | solution.py:849
  348.4 3.9 collective-permute-done.28
  354.2 5.0 %collective-permute-done.29 = f32[16,128]{1,0:T(8,128)S(1)} collective-permute-done((f32[16,128]{1,0:T(8,128)S(1)}, f32[16,128]{1,0:T(8,128)S(1)}, u32[]{:S(2)}, u32[]{:S(2)}) %collective-permute-start.29) | collective-permute-done | bytes 8224 | tf_op jit(solution)/shard_map/ppermute | solution.py:118
  360.2 4.3 %all-to-all-start.4 = ((bf16[16,16,1664]{2,1,0:T(8,128)(2,1)}), bf16[16,16,1664]{2,1,0:T(8,128)(2,1)}, u32[]{:S(2)}, u32[]{:S(2)}) async-start(bf16[16,16,1664]{2,1,0:T(8,128)(2,1)} %broadcast_in_dim.13), calls=%async_computation.4 | async-start | bytes 1703936 | tf_op jit(solution)/shard_map/all_to_all | solution.py:865
  367.8 7.5 %all-to-all-done.4 = bf16[16,16,1664]{2,1,0:T(8,128)(2,1)} async-done(((bf16[16,16,1664]{2,1,0:T(8,128)(2,1)}), bf16[16,16,1664]{2,1,0:T(8,128)(2,1)}, u32[]{:S(2)}, u32[]{:S(2)}) %all-to-all-start.4) | async-done | bytes 852000 | tf_op jit(solution)/shard_map/all_to_all | solution.py:865
  375.3 5.8 %collective-permute-start.33 = (bf16[16,16,1664]{2,1,0:T(8,128)(2,1)}, bf16[16,16,1664]{2,1,0:T(8,128)(2,1)S(1)}, u32[]{:S(2)}, u32[]{:S(2)}) collective-permute-start(bf16[16,16,1664]{2,1,0:T(8,128)(2,1)} %all-to-all-done.4), channel_id=1, source_target_pairs={{0,128},{128,0},{1,129},{129,1},{2,130},{130,2},{3,131},{131,3},{4... | collective-permute-start | bytes 2555912 | tf_op jit(solution)/shard_map/ppermute | solution.py:128
  (208 shorter events, 126.0 us)
Async XLA Ops:
  7.2 63.4 %all-gather.11.cloned.1.call-start = ((), (), s32[]{:S(2)}) async-start(), calls=%async_computation.9 | async-start | bytes 4866048 | tf_op jit(solution)/shard_map/all_gather | solution.py:738
  10.6 131.6 %all-gather.7.cloned.1.call-start = ((), (), s32[]{:S(2)}) async-start(), calls=%async_computation.6 | async-start | bytes 10027008 | tf_op jit(solution)/shard_map/all_gather | solution.py:766
  26.8 22.6 %collective-permute-start.3 = (bf16[4,128,1664]{2,1,0:T(8,128)(2,1)}, bf16[4,128,1664]{2,1,0:T(8,128)(2,1)}, u32[]{:S(2)}, u32[]{:S(2)}) collective-permute-start(bf16[4,128,1664]{2,1,0:T(8,128)(2,1)} %pad_maximum_fusion.1.refs_1_), channel_id=1, source_target_pairs={{0,32},{8,40},{16,48},{24,56},{32,64},{40,72},{48,80},{56,88},{64,... | collective-permute-start | bytes 5111816 | tf_op jit(solution)/shard_map/ppermute | solution.py:65
  28.1 21.3 %collective-permute-start.4 = (bf16[4,128,1664]{2,1,0:T(8,128)(2,1)}, bf16[4,128,1664]{2,1,0:T(8,128)(2,1)}, u32[]{:S(2)}, u32[]{:S(2)}) collective-permute-start(bf16[4,128,1664]{2,1,0:T(8,128)(2,1)} %pad_maximum_fusion.1.refs_1_), channel_id=1, source_target_pairs={{0,96},{8,104},{16,112},{24,120},{32,0},{40,8},{48,16},{56,24},{64... | collective-permute-start | bytes 5111816 | tf_op jit(solution)/shard_map/ppermute | solution.py:65
  29.6 39.3 %collective-permute-start.5 = (bf16[4,128,1664]{2,1,0:T(8,128)(2,1)}, bf16[4,128,1664]{2,1,0:T(8,128)(2,1)}, u32[]{:S(2)}, u32[]{:S(2)}) collective-permute-start(bf16[4,128,1664]{2,1,0:T(8,128)(2,1)} %pad_maximum_fusion.1.refs_1_), channel_id=1, source_target_pairs={{0,64},{8,72},{16,80},{24,88},{32,96},{40,104},{48,112},{56,120},{... | collective-permute-start | bytes 5111816 | tf_op jit(solution)/shard_map/ppermute | solution.py:65
  76.1 20.8 %collective-permute-start.6 = (bf16[8,48,1536]{2,1,0:T(8,128)(2,1)}, bf16[8,48,1536]{2,1,0:T(8,128)(2,1)}, u32[]{:S(2)}, u32[]{:S(2)}) collective-permute-start(bf16[8,48,1536]{2,1,0:T(8,128)(2,1)} %get-tuple-element.246), channel_id=1, source_target_pairs={{0,8},{8,16},{16,24},{24,0},{32,40},{40,48},{48,56},{56,32},{64,72... | collective-permute-start | bytes 3538952 | tf_op jit(solution)/shard_map/ppermute | solution.py:65
  77.3 27.6 %collective-permute-start.7 = (bf16[8,48,1536]{2,1,0:T(8,128)(2,1)}, bf16[8,48,1536]{2,1,0:T(8,128)(2,1)}, u32[]{:S(2)}, u32[]{:S(2)}) collective-permute-start(bf16[8,48,1536]{2,1,0:T(8,128)(2,1)} %get-tuple-element.246), channel_id=1, source_target_pairs={{0,24},{8,0},{16,8},{24,16},{32,56},{40,32},{48,40},{56,48},{64,88... | collective-permute-start | bytes 3538952 | tf_op jit(solution)/shard_map/ppermute | solution.py:65
  78.8 28.5 %collective-permute-start.8 = (bf16[8,48,1536]{2,1,0:T(8,128)(2,1)}, bf16[8,48,1536]{2,1,0:T(8,128)(2,1)S(1)}, u32[]{:S(2)}, u32[]{:S(2)}) collective-permute-start(bf16[8,48,1536]{2,1,0:T(8,128)(2,1)} %get-tuple-element.246), channel_id=1, source_target_pairs={{0,16},{8,24},{16,0},{24,8},{32,48},{40,56},{48,32},{56,40},{64,80... | collective-permute-start | bytes 3538952 | tf_op jit(solution)/shard_map/ppermute | solution.py:65
  90.9 23.6 %all-to-all-start = ((bf16[8,192,128]{2,1,0:T(8,128)(2,1)}), bf16[8,192,128]{2,1,0:T(8,128)(2,1)S(1)}, u32[]{:S(2)}, u32[]{:S(2)}) async-start(bf16[8,192,128]{2,1,0:T(8,128)(2,1)} %get-tuple-element.133), calls=%async_computation | async-start | bytes 786432 | tf_op jit(solution)/shard_map/all_to_all | solution.py:770
  96.9 119.0 %all-gather.13.cloned.1.call-start = ((), (), s32[]{:S(2)}) async-start(), calls=%async_computation.10 | async-start | bytes 4423680 | tf_op jit(solution)/shard_map/all_gather | solution.py:777
  114.5 185.1 %all-gather.9.cloned.1.call-start = ((), (), s32[]{:S(2)}) async-start(), calls=%async_computation.7 | async-start | bytes 3538944 | tf_op jit(solution)/shard_map/all_gather | solution.py:826
  133.5 22.5 %collective-permute-start.12 = (bf16[4,128,1664]{2,1,0:T(8,128)(2,1)}, bf16[4,128,1664]{2,1,0:T(8,128)(2,1)}, u32[]{:S(2)}, u32[]{:S(2)}) collective-permute-start(bf16[4,128,1664]{2,1,0:T(8,128)(2,1)} %pad_maximum_fusion.2.refs_0_), channel_id=1, source_target_pairs={{0,32},{8,40},{16,48},{24,56},{32,64},{40,72},{48,80},{56,88},{64,... | collective-permute-start | bytes 5111816 | tf_op jit(solution)/shard_map/ppermute | solution.py:65
  134.8 21.7 %collective-permute-start.13 = (bf16[4,128,1664]{2,1,0:T(8,128)(2,1)}, bf16[4,128,1664]{2,1,0:T(8,128)(2,1)S(1)}, u32[]{:S(2)}, u32[]{:S(2)}) collective-permute-start(bf16[4,128,1664]{2,1,0:T(8,128)(2,1)} %pad_maximum_fusion.2.refs_0_), channel_id=1, source_target_pairs={{0,96},{8,104},{16,112},{24,120},{32,0},{40,8},{48,16},{56,24},{64... | collective-permute-start | bytes 5111816 | tf_op jit(solution)/shard_map/ppermute | solution.py:65
  156.5 24.0 %collective-permute-start.16 = (bf16[4,128,1664]{2,1,0:T(8,128)(2,1)}, bf16[4,128,1664]{2,1,0:T(8,128)(2,1)S(1)}, u32[]{:S(2)}, u32[]{:S(2)}) collective-permute-start(bf16[4,128,1664]{2,1,0:T(8,128)(2,1)} %pad_maximum_fusion.2.refs_0_), channel_id=1, source_target_pairs={{0,64},{8,72},{16,80},{24,88},{32,96},{40,104},{48,112},{56,120},{... | collective-permute-start | bytes 5111816 | tf_op jit(solution)/shard_map/ppermute | solution.py:65
  178.4 39.3 %collective-permute-start.14 = (bf16[4,128,1664]{2,1,0:T(8,128)(2,1)}, bf16[4,128,1664]{2,1,0:T(8,128)(2,1)}, u32[]{:S(2)}, u32[]{:S(2)}) collective-permute-start(bf16[4,128,1664]{2,1,0:T(8,128)(2,1)} %get-tuple-element.153), channel_id=1, source_target_pairs={{0,96},{8,104},{16,112},{24,120},{32,0},{40,8},{48,16},{56,24},{64... | collective-permute-start | bytes 5111816 | tf_op jit(solution)/shard_map/ppermute | solution.py:65
  180.3 40.9 %collective-permute-start.15 = (bf16[4,128,1664]{2,1,0:T(8,128)(2,1)}, bf16[4,128,1664]{2,1,0:T(8,128)(2,1)}, u32[]{:S(2)}, u32[]{:S(2)}) collective-permute-start(bf16[4,128,1664]{2,1,0:T(8,128)(2,1)} %get-tuple-element.154), channel_id=1, source_target_pairs={{0,32},{8,40},{16,48},{24,56},{32,64},{40,72},{48,80},{56,88},{64,... | collective-permute-start | bytes 5111816 | tf_op jit(solution)/shard_map/ppermute | solution.py:65
  193.8 27.5 %collective-permute-start.17 = (bf16[4,128,1664]{2,1,0:T(8,128)(2,1)}, bf16[4,128,1664]{2,1,0:T(8,128)(2,1)}, u32[]{:S(2)}, u32[]{:S(2)}) collective-permute-start(bf16[4,128,1664]{2,1,0:T(8,128)(2,1)} %get-tuple-element.163), channel_id=1, source_target_pairs={{0,64},{8,72},{16,80},{24,88},{32,96},{40,104},{48,112},{56,120},{... | collective-permute-start | bytes 5111816 | tf_op jit(solution)/shard_map/ppermute | solution.py:65
  221.2 18.5 %collective-permute-start.19 = (bf16[6,768,512]{2,1,0:T(8,128)(2,1)}, bf16[6,768,512]{2,1,0:T(8,128)(2,1)S(1)}, u32[]{:S(2)}, u32[]{:S(2)}) collective-permute-start(bf16[6,768,512]{2,1,0:T(8,128)(2,1)} %shard_map.253), channel_id=1, source_target_pairs={{0,128},{128,0},{1,129},{129,1},{2,130},{130,2},{3,131},{131,3},{4... | collective-permute-start | bytes 14155784 | tf_op jit(solution)/shard_map/ppermute | solution.py:128
  232.5 13.1 %collective-permute-start.20 = (bf16[128,1664]{1,0:T(8,128)(2,1)S(1)}, bf16[128,1664]{1,0:T(8,128)(2,1)S(1)}, u32[]{:S(2)}, u32[]{:S(2)}) collective-permute-start(bf16[128,1664]{1,0:T(8,128)(2,1)S(1)} %get-tuple-element.200), channel_id=1, source_target_pairs={{0,8},{8,16},{16,24},{24,0},{32,40},{40,48},{48,56},{56,32},{64,72... | collective-permute-start | bytes 1277960 | tf_op jit(solution)/shard_map/ppermute | solution.py:65
  233.9 11.7 %collective-permute-start.21 = (bf16[128,1664]{1,0:T(8,128)(2,1)S(1)}, bf16[128,1664]{1,0:T(8,128)(2,1)S(1)}, u32[]{:S(2)}, u32[]{:S(2)}) collective-permute-start(bf16[128,1664]{1,0:T(8,128)(2,1)S(1)} %get-tuple-element.201), channel_id=1, source_target_pairs={{0,16},{8,24},{16,0},{24,8},{32,48},{40,56},{48,32},{56,40},{64,80... | collective-permute-start | bytes 1277960 | tf_op jit(solution)/shard_map/ppermute | solution.py:65
  253.0 19.3 %all-to-all-start.1 = ((bf16[8,192,128]{2,1,0:T(8,128)(2,1)}), bf16[8,192,128]{2,1,0:T(8,128)(2,1)S(1)}, u32[]{:S(2)}, u32[]{:S(2)}) async-start(bf16[8,192,128]{2,1,0:T(8,128)(2,1)} %bitcast.25), calls=%async_computation.1 | async-start | bytes 786432 | tf_op jit(solution)/shard_map/all_to_all | solution.py:820
  256.5 53.8 %collective-permute-start.23 = (bf16[4,128,1536]{2,1,0:T(8,128)(2,1)}, bf16[4,128,1536]{2,1,0:T(8,128)(2,1)S(1)}, u32[]{:S(2)}, u32[]{:S(2)}) collective-permute-start(bf16[4,128,1536]{2,1,0:T(8,128)(2,1)} %get-tuple-element.219), channel_id=1, source_target_pairs={{0,96},{8,104},{16,112},{24,120},{32,0},{40,8},{48,16},{56,24},{64... | collective-permute-start | bytes 4718600 | tf_op jit(solution)/shard_map/ppermute | solution.py:65
  257.7 52.6 %collective-permute-start.24 = (bf16[4,128,1536]{2,1,0:T(8,128)(2,1)}, bf16[4,128,1536]{2,1,0:T(8,128)(2,1)}, u32[]{:S(2)}, u32[]{:S(2)}) collective-permute-start(bf16[4,128,1536]{2,1,0:T(8,128)(2,1)} %get-tuple-element.220), channel_id=1, source_target_pairs={{0,32},{8,40},{16,48},{24,56},{32,64},{40,72},{48,80},{56,88},{64,... | collective-permute-start | bytes 4718600 | tf_op jit(solution)/shard_map/ppermute | solution.py:65
  258.1 52.2 %collective-permute-start.25 = (bf16[4,128,1536]{2,1,0:T(8,128)(2,1)}, bf16[4,128,1536]{2,1,0:T(8,128)(2,1)}, u32[]{:S(2)}, u32[]{:S(2)}) collective-permute-start(bf16[4,128,1536]{2,1,0:T(8,128)(2,1)} %get-tuple-element.221), channel_id=1, source_target_pairs={{0,64},{8,72},{16,80},{24,88},{32,96},{40,104},{48,112},{56,120},{... | collective-permute-start | bytes 4718600 | tf_op jit(solution)/shard_map/ppermute | solution.py:65
  292.8 25.1 %all-to-all-start.2 = ((bf16[8,320,128]{2,1,0:T(8,128)(2,1)}), bf16[8,320,128]{2,1,0:T(8,128)(2,1)S(1)}, u32[]{:S(2)}, u32[]{:S(2)}) async-start(bf16[8,320,128]{2,1,0:T(8,128)(2,1)} %get-tuple-element.216), calls=%async_computation.2 | async-start | bytes 1310720 | tf_op jit(solution)/shard_map/all_to_all | solution.py:825
  299.5 75.8 %reduce-scatter.2.cloned.1.call-start = ((), (), s32[]{:S(2)}) async-start(), calls=%async_computation.8 | async-start | bytes 5308416 | tf_op jit(solution)/shard_map/reduce_scatter | solution.py:846
  318.8 14.9 %collective-permute-start.26 = (bf16[8,160,1536]{2,1,0:T(8,128)(2,1)}, bf16[8,160,1536]{2,1,0:T(8,128)(2,1)}, u32[]{:S(2)}, u32[]{:S(2)}) collective-permute-start(bf16[8,160,1536]{2,1,0:T(8,128)(2,1)} %bitcast.100), channel_id=1, source_target_pairs={{0,128},{128,0},{1,129},{129,1},{2,130},{130,2},{3,131},{131,3},{4... | collective-permute-start | bytes 11796488 | tf_op jit(solution)/shard_map/ppermute | solution.py:128
  324.3 18.7 %all-to-all-start.3 = ((bf16[16,16,1664]{2,1,0:T(8,128)(2,1)}), bf16[16,16,1664]{2,1,0:T(8,128)(2,1)}, u32[]{:S(2)}, u32[]{:S(2)}) async-start(bf16[16,16,1664]{2,1,0:T(8,128)(2,1)} %fusion.1), calls=%async_computation.3 | async-start | bytes 1703936 | tf_op jit(solution)/shard_map/all_to_all | solution.py:849
  344.7 21.7 %collective-permute-start.32 = (bf16[128,1536]{1,0:T(8,128)(2,1)}, bf16[128,1536]{1,0:T(8,128)(2,1)}, u32[]{:S(2)}, u32[]{:S(2)}) collective-permute-start(bf16[128,1536]{1,0:T(8,128)(2,1)} %copy-done.15), channel_id=1, source_target_pairs={{0,16},{8,24},{16,0},{24,8},{32,48},{40,56},{48,32},{56,40},{64,80... | collective-permute-start | bytes 1179656 | tf_op jit(solution)/shard_map/ppermute | solution.py:65
  345.6 20.8 %collective-permute-start.31 = (bf16[128,1536]{1,0:T(8,128)(2,1)}, bf16[128,1536]{1,0:T(8,128)(2,1)}, u32[]{:S(2)}, u32[]{:S(2)}) collective-permute-start(bf16[128,1536]{1,0:T(8,128)(2,1)} %copy-done.14), channel_id=1, source_target_pairs={{0,8},{8,16},{16,24},{24,0},{32,40},{40,48},{48,56},{56,32},{64,72... | collective-permute-start | bytes 1179656 | tf_op jit(solution)/shard_map/ppermute | solution.py:65
  346.3 20.0 %collective-permute-start.30 = (bf16[128,1536]{1,0:T(8,128)(2,1)S(1)}, bf16[128,1536]{1,0:T(8,128)(2,1)}, u32[]{:S(2)}, u32[]{:S(2)}) collective-permute-start(bf16[128,1536]{1,0:T(8,128)(2,1)S(1)} %get-tuple-element.236), channel_id=1, source_target_pairs={{0,24},{8,0},{16,8},{24,16},{32,56},{40,32},{48,40},{56,48},{64,88... | collective-permute-start | bytes 1179656 | tf_op jit(solution)/shard_map/ppermute | solution.py:65
  360.2 15.1 %all-to-all-start.4 = ((bf16[16,16,1664]{2,1,0:T(8,128)(2,1)}), bf16[16,16,1664]{2,1,0:T(8,128)(2,1)}, u32[]{:S(2)}, u32[]{:S(2)}) async-start(bf16[16,16,1664]{2,1,0:T(8,128)(2,1)} %broadcast_in_dim.13), calls=%async_computation.4 | async-start | bytes 1703936 | tf_op jit(solution)/shard_map/all_to_all | solution.py:865
  (47 other events, 327.9 us)
Sparse Core Ops, SparseCore 0:
  10.7 59.8 all-gather.10
  73.0 69.1 all-gather.6
  144.0 50.4 all-gather.12
  253.2 45.3 all-gather.8
  318.1 56.7 reduce-scatter.1
where the time goes:
time: 404 us; the launch traced here: 396 us
  Pallas kernels  128 us (32%)
  waiting for transfers between devices  119 us (29%)
  starting transfers between devices  79.3 us (20%)
  other arithmetic  26.1 us (6%)
  local copies, waits for them, and re-layouts  25.3 us (6%)
  between operations  14.7 us (4%)
    ppermute x27, waiting for transfers between devices, cross(): return lax.ppermute(values, ('dp', 'expert'), pairs)  76.2 us
    pallas_call x3, Pallas kernels, run_experts(): pl.pallas_call(functools.partial(expert_kernel, groups), grid=(2,), out_s...  44 us
    ppermute x27, starting transfers between devices, cross(): return lax.ppermute(values, ('dp', 'expert'), pairs)  34.4 us
    pallas_call x2, Pallas kernels, run_weight_grads(): pl.pallas_call(functools.partial(weight_grad_kernel, len(saved)), grid=(2...  22.8 us
    ppermute x4, starting transfers between devices, swap_cores(): return lax.ppermute(values, 'dp', [(0, 1), (1, 0)])  18.3 us
    pallas_call x1, Pallas kernels, run_attention_back(): pl.pallas_call(attention_back_kernel, out_shape=(jax.ShapeDtypeStruct((se...  13.5 us
    pallas_call x1, Pallas kernels, run_attention(): pl.pallas_call(attention_kernel, out_shape=(jax.ShapeDtypeStruct((seq_len...  10.5 us
    pallas_call x1, Pallas kernels, run_mixture(): pl.pallas_call(functools.partial(mixture_kernel, groups), grid=(2,), out_...  10.3 us
  transfers between devices with their start and end apart: 44, of which 22 were waited for; matrix products, arithmetic and copies ran while one was open for 10% of the time, Pallas kernels for 31%

commit v1 on v0

--- a/solution.py
+++ b/solution.py
@@ -821,6 +821,7 @@
         context_grad.reshape(planes, query_width, tok_rows), "tensor", split_axis=0, concat_axis=0
     )
     context_grad, kept = together(context_grad, kept)
+    weight_sum = lax.psum_scatter(kept, "tensor", scatter_dimension=1, tiled=True)
     joined_grad, joined_blocks = run_attention_back(qkv, context_grad, marks, tables)
     joined_home = lax.all_to_all(joined_blocks, "tensor", split_axis=0, concat_axis=0)
     attention_all = lax.all_gather(attention_low, "tensor", axis=0, tiled=True)
@@ -840,10 +841,9 @@
     def of_core(which):
         return lax.dynamic_index_in_dim(blocks, which, 0, keepdims=False)
 
-    blocks, theirs, joined_home, kept, *mix_arrived = together(
-        blocks, swap_cores(of_core(1 - core)), joined_home, kept, *mix_arrived
-    )
-    weight_sum = lax.psum_scatter(kept, "tensor", scatter_dimension=1, tiled=True)
+    blocks, theirs, joined_home, *mix_arrived = together(
+        blocks, swap_cores(of_core(1 - core)), joined_home, *mix_arrived
+    )
 
     part = of_core(core).astype(f32) + theirs.astype(f32)
     arrived = lax.all_to_all(part.astype(bf16), "expert", split_axis=0, concat_axis=0)

time: 404 us -> 410 us (1.015)
  waiting for transfers between devices: 119 us -> 131 us
    all_to_all x1, waiting for transfers between devices: 7.66 us -> 13.6 us  [local(): lax.all_to_all(joined_blocks, 'tensor', split_axis=0, concat_axis=0)]
  transfers between devices with their start and end apart: 44 -> 44, of which waited for: 22 -> 24; matrix products, arithmetic and copies ran while one was open for 10% -> 10% of each run, Pallas kernels for 31% -> 30%
where the time goes in v1:
time: 410 us; the launch traced here: 402 us
  waiting for transfers between devices  131 us (32%)
  Pallas kernels  127 us (31%)
  starting transfers between devices  75.5 us (18%)
  other arithmetic  26.2 us (6%)
  local copies, waits for them, and re-layouts  23 us (6%)
  between operations  14.7 us (4%)
    ppermute x27, waiting for transfers between devices, cross(): return lax.ppermute(values, ('dp', 'expert'), pairs)  79.3 us
    pallas_call x3, Pallas kernels, run_experts(): pl.pallas_call(functools.partial(expert_kernel, groups), grid=(2,), out_s...  44 us
    ppermute x27, starting transfers between devices, cross(): return lax.ppermute(values, ('dp', 'expert'), pairs)  34 us
    pallas_call x2, Pallas kernels, run_weight_grads(): pl.pallas_call(functools.partial(weight_grad_kernel, len(saved)), grid=(2...  22.5 us
    ppermute x4, starting transfers between devices, swap_cores(): return lax.ppermute(values, 'dp', [(0, 1), (1, 0)])  19.4 us
    all_to_all x1, waiting for transfers between devices, local(): lax.all_to_all(joined_blocks, 'tensor', split_axis=0, concat_axis=0)  13.6 us
    pallas_call x1, Pallas kernels, run_attention_back(): pl.pallas_call(attention_back_kernel, out_shape=(jax.ShapeDtypeStruct((se...  13.5 us
    pallas_call x1, Pallas kernels, run_attention(): pl.pallas_call(attention_kernel, out_shape=(jax.ShapeDtypeStruct((seq_len...  10.5 us
  transfers between devices with their start and end apart: 44, of which 24 were waited for; matrix products, arithmetic and copies ran while one was open for 10% of the time, Pallas kernels for 30%

profile of v1, /device:TPU:1, one launch (start us, length us, event | category | flops | bytes accessed | tf_op | source)
XLA Modules:
  0.0 402.1 jit_solution(8107425092255865337)
XLA Ops:
  16.0 4.3 %collective-permute-done.2 = bf16[128,1664]{1,0:T(8,128)(2,1)S(1)} collective-permute-done((bf16[128,1664]{1,0:T(8,128)(2,1)S(1)}, bf16[128,1664]{1,0:T(8,128)(2,1)S(1)}, u32[]{:S(2)}, u32[]{:S(2)}) %collective-permute-start.2) | collective-permute-done | bytes 426016 | tf_op jit(solution)/shard_map/ppermute | solution.py:65
  20.4 4.9 %collective-permute-done.1 = bf16[128,1664]{1,0:T(8,128)(2,1)S(1)} collective-permute-done((bf16[128,1664]{1,0:T(8,128)(2,1)S(1)}, bf16[128,1664]{1,0:T(8,128)(2,1)S(1)}, u32[]{:S(2)}, u32[]{:S(2)}) %collective-permute-start.1) | collective-permute-done | bytes 426016 | tf_op jit(solution)/shard_map/ppermute | solution.py:65
  36.1 13.3 %collective-permute-done.3.refs_2_ = bf16[4,128,1664]{2,1,0:T(8,128)(2,1)} collective-permute-done((bf16[4,128,1664]{2,1,0:T(8,128)(2,1)}, bf16[4,128,1664]{2,1,0:T(8,128)(2,1)}, u32[]{:S(2)}, u32[]{:S(2)}) %collective-permute-start.3) | collective-permute-done | bytes 1703968 | tf_op jit(solution)/shard_map/ppermute | solution.py:65
  49.4 19.4 %collective-permute-done.5.refs_1_ = bf16[4,128,1664]{2,1,0:T(8,128)(2,1)} collective-permute-done((bf16[4,128,1664]{2,1,0:T(8,128)(2,1)}, bf16[4,128,1664]{2,1,0:T(8,128)(2,1)}, u32[]{:S(2)}, u32[]{:S(2)}) %collective-permute-start.5) | collective-permute-done | bytes 1703968 | tf_op jit(solution)/shard_map/ppermute | solution.py:65
  80.4 10.5 %shard_map.247 = (bf16[1024,192]{1,0:T(8,128)(2,1)}, bf16[8,192,128]{2,1,0:T(8,128)(2,1)}, bf16[1024,320]{1,0:T(8,128)(2,1)}) custom-call(bf16[8,176,1536]{2,1,0:T(8,128)(2,1)} %bitcast.96, bf16[320,1536]{1,0:T(8,128)(2,1)} %copy-done.14, s32[1024,1]{1,0:T(8,128)} %compare_select_fusion.col_ref, s32[1,1024]{1,0:T(1,128)} %compare_select_fusion.1.row_ref, ...), custom_call_target="tpu_custom_call" | custom-call | flops 268435456 | bytes 1048576 | tf_op jit(solution)/shard_map/pallas_call | solution.py:246
  90.9 6.0 %all-to-all-start = ((bf16[8,192,128]{2,1,0:T(8,128)(2,1)}), bf16[8,192,128]{2,1,0:T(8,128)(2,1)S(1)}, u32[]{:S(2)}, u32[]{:S(2)}) async-start(bf16[8,192,128]{2,1,0:T(8,128)(2,1)} %get-tuple-element.132), calls=%async_computation | async-start | bytes 786432 | tf_op jit(solution)/shard_map/all_to_all | solution.py:770
  99.3 5.6 %collective-permute-done.7 = bf16[8,48,1536]{2,1,0:T(8,128)(2,1)} collective-permute-done((bf16[8,48,1536]{2,1,0:T(8,128)(2,1)}, bf16[8,48,1536]{2,1,0:T(8,128)(2,1)}, u32[]{:S(2)}, u32[]{:S(2)}) %collective-permute-start.7) | collective-permute-done | bytes 1179680 | tf_op jit(solution)/shard_map/ppermute | solution.py:65
  108.4 6.1 %all-to-all-done = bf16[8,192,128]{2,1,0:T(8,128)(2,1)S(1)} async-done(((bf16[8,192,128]{2,1,0:T(8,128)(2,1)}), bf16[8,192,128]{2,1,0:T(8,128)(2,1)S(1)}, u32[]{:S(2)}, u32[]{:S(2)}) %all-to-all-start) | async-done | bytes 393248 | tf_op jit(solution)/shard_map/all_to_all | solution.py:770
  122.5 4.7 %collective-permute-done.11 = bf16[128,1664]{1,0:T(8,128)(2,1)S(1)} collective-permute-done((bf16[128,1664]{1,0:T(8,128)(2,1)S(1)}, bf16[128,1664]{1,0:T(8,128)(2,1)S(1)}, u32[]{:S(2)}, u32[]{:S(2)}) %collective-permute-start.11) | collective-permute-done | bytes 426016 | tf_op jit(solution)/shard_map/ppermute | solution.py:65
  136.5 5.7 %all-gather.7.cloned.1.call-done.refs_2_.refs_4_.refs_6_ = bf16[6,1536,512]{2,1,0:T(8,128)(2,1)} async-done(((bf16[6,96,512]{2,1,0:T(8,128)(2,1)}), bf16[6,1536,512]{2,1,0:T(8,128)(2,1)}) %all-gather.7.cloned.1.call-update) | async-done | bytes 9437200 | tf_op jit(solution)/shard_map/all_gather | solution.py:766
  142.2 12.0 %shard_map.249 = (bf16[4,128,1664]{2,1,0:T(8,128)(2,1)}, bf16[2,256,1536]{2,1,0:T(8,128)(2,1)}, bf16[2,256,1536]{2,1,0:T(8,128)(2,1)}, bf16[2,256,512]{2,1,0:T(8...) custom-call(s32[1]{0:T(128)} %bitcast.18.first_ref, ...), custom_call_target="tpu_custom_call" | custom-call | flops 4831838208 | bytes 25165824 | tf_op jit(solution)/shard_map/pallas_call | solution.py:488
  158.3 20.1 %shard_map.250 = (bf16[4,128,1664]{2,1,0:T(8,128)(2,1)}, bf16[4,128,1664]{2,1,0:T(8,128)(2,1)}, bf16[2,512,1536]{2,1,0:T(8,128)(2,1)}, bf16[2,512,1536]{2,1,0:T(...) custom-call(s32[1]{0:T(128)} %bitcast.18.first_ref, ...), custom_call_target="tpu_custom_call" | custom-call | flops 9663676416 | bytes 25165824 | tf_op jit(solution)/shard_map/pallas_call | solution.py:488
  181.7 12.0 %shard_map.251 = (bf16[4,128,1664]{2,1,0:T(8,128)(2,1)}, bf16[2,256,1536]{2,1,0:T(8,128)(2,1)}, bf16[2,256,1536]{2,1,0:T(8,128)(2,1)}, bf16[2,256,512]{2,1,0:T(8...) custom-call(s32[1]{0:T(128)} %bitcast.18.first_ref, ...), custom_call_target="tpu_custom_call" | custom-call | flops 4831838208 | bytes 25165824 | tf_op jit(solution)/shard_map/pallas_call | solution.py:488
  195.1 10.4 %shard_map.253 = bf16[6,768,512]{2,1,0:T(8,128)(2,1)} custom-call(s32[1]{0:T(128)} %bitcast.23.half_ref, bf16[2,256,1536]{2,1,0:T(8,128)(2,1)} %get-tuple-element.173.refs_0_, bf16[2,512,1536]{2,1,0:T(8,128)(2,1)} %get-tuple-element.174.refs_1_, bf16[2,256,1536]{2,1,0:T(8,128)(2,1)} %get-tuple-element.175.refs_2_, ...), custom_call_target="tpu_custom_call" | custom-call | flops 268435456 | bytes 1048576 | tf_op jit(solution)/shard_map/pallas_call | solution.py:626
  205.6 10.2 %shard_map.252 = (bf16[4,128,1536]{2,1,0:T(8,128)(2,1)}, bf16[4,128,1536]{2,1,0:T(8,128)(2,1)}, bf16[4,128,1536]{2,1,0:T(8,128)(2,1)}, bf16[4,128,1536]{2,1,0:T(8,128)(2,1)}) custom-call(bf16[4,128,128]{2,1,0:T(8,128)(2,1)} %get-tuple-element.163.refs_0_, bf16[8,128,128]{2,1,0:T(8,128)(2,1)} %get-tuple-element.164.refs_1_, ...), custom_call_target="tpu_custom_call" | custom-call | flops 4294967296 | bytes 1048576 | tf_op jit(solution)/shard_map/pallas_call | solution.py:563
  221.2 7.3 %collective-permute-start.19 = (bf16[6,768,512]{2,1,0:T(8,128)(2,1)}, bf16[6,768,512]{2,1,0:T(8,128)(2,1)S(1)}, u32[]{:S(2)}, u32[]{:S(2)}) collective-permute-start(bf16[6,768,512]{2,1,0:T(8,128)(2,1)} %shard_map.253), channel_id=1, source_target_pairs={{0,128},{128,0},{1,129},{129,1},{2,130},{130,2},{3,131},{131,3},{4... | collective-permute-start | bytes 14155784 | tf_op jit(solution)/shard_map/ppermute | solution.py:128
  234.2 5.5 %collective-permute-done.18.refs_1_ = bf16[128,1664]{1,0:T(8,128)(2,1)S(1)} collective-permute-done((bf16[128,1664]{1,0:T(8,128)(2,1)S(1)}, bf16[128,1664]{1,0:T(8,128)(2,1)S(1)}, u32[]{:S(2)}, u32[]{:S(2)}) %collective-permute-start.18) | collective-permute-done | bytes 426016 | tf_op jit(solution)/shard_map/ppermute | solution.py:65
  239.7 5.9 %collective-permute-done.20.refs_2_ = bf16[128,1664]{1,0:T(8,128)(2,1)S(1)} collective-permute-done((bf16[128,1664]{1,0:T(8,128)(2,1)S(1)}, bf16[128,1664]{1,0:T(8,128)(2,1)S(1)}, u32[]{:S(2)}, u32[]{:S(2)}) %collective-permute-start.20) | collective-permute-done | bytes 426016 | tf_op jit(solution)/shard_map/ppermute | solution.py:65
  245.6 5.3 %shard_map.255 = (f32[128,1536]{1,0:T(8,128)S(1)}, bf16[128,1536]{1,0:T(8,128)(2,1)}, bf16[1536,128]{1,0:T(8,128)(2,1)}, bf16[128,32]{1,0:T(8,128)(2,1)S(1)}, f32[1,1536]{1,0:T(1,128)S(1)}) custom-call(bf16[128,1664]{1,0:T(8,128)(2,1)S(1)} %get-tuple-element.197.refs_0_, bf16[128,1664]{1,0:T(8,128)(2,1)S(1)} %collective-permute-done.18.refs_1_, ...), custom_call_target="tpu_custom_call" | custom-call | flops 1073741824 | bytes 8388608 | tf_op jit(solution)/shard_map/pallas_call | solution.py:443
  256.5 12.1 %shard_map.256 = bf16[6,768,512]{2,1,0:T(8,128)(2,1)} custom-call(s32[1]{0:T(128)} %bitcast.26.half_ref, bf16[2,256,1536]{2,1,0:T(8,128)(2,1)} %get-tuple-element.173.refs_0_, bf16[2,512,1536]{2,1,0:T(8,128)(2,1)} %get-tuple-element.174.refs_1_, bf16[2,256,1536]{2,1,0:T(8,128)(2,1)} %get-tuple-element.175.refs_2_, ...), custom_call_target="tpu_custom_call" | custom-call | flops 268435456 | bytes 1048576 | tf_op jit(solution)/shard_map/pallas_call | solution.py:626
  270.9 6.1 %collective-permute-start.26 = (bf16[8,160,1536]{2,1,0:T(8,128)(2,1)}, bf16[8,160,1536]{2,1,0:T(8,128)(2,1)}, u32[]{:S(2)}, u32[]{:S(2)}) collective-permute-start(bf16[8,160,1536]{2,1,0:T(8,128)(2,1)} %bitcast.100), channel_id=1, source_target_pairs={{0,128},{128,0},{1,129},{129,1},{2,130},{130,2},{3,131},{131,3},{4... | collective-permute-start | bytes 11796488 | tf_op jit(solution)/shard_map/ppermute | solution.py:128
  279.7 13.5 %shard_map.257 = (bf16[1024,320]{1,0:T(8,128)(2,1)}, bf16[8,320,128]{2,1,0:T(8,128)(2,1)}) custom-call(bf16[1024,320]{1,0:T(8,128)(2,1)} %get-tuple-element.138.qkv_ref, bf16[8,192,128]{2,1,0:T(8,128)(2,1)} %copy-done.19, s32[1024,1]{1,0:T(8,128)} %compare_select_fusion.col_ref, s32[1,1024]{1,0:T(1,128)} %compare_select_fusion.1.row_ref, ...), custom_call_target="tpu_custom_call" | custom-call | flops 268435456 | bytes 1048576 | tf_op jit(solution)/shard_map/pallas_call | solution.py:266
  293.1 5.2 %shard_map.258 = (bf16[320,1536]{1,0:T(8,128)(2,1)}, bf16[34,1536]{1,0:T(8,128)(2,1)}) custom-call(bf16[8,176,1536]{2,1,0:T(8,128)(2,1)} %bitcast.97, bf16[1024,320]{1,0:T(8,128)(2,1)} %get-tuple-element.208.grad_ref, bf16[320,1536]{1,0:T(8,128)(2,1)} %copy-done.14, bf16[128,1664]{1,0:T(8,128)(2,1)} %copy-done.3, bf16[128,32]{1,0:T(8,128)(2,1)} %copy-done.10, ...), custom_call_target="tpu_custom_call" | custom-call | flops 1048576 | bytes 65536 | tf_op jit(solution)/shard_map/pallas_call | solution.py:660
  303.2 4.7 %shard_map.259 = bf16[192,1536]{1,0:T(8,128)(2,1)} custom-call(bf16[1024,1536]{1,0:T(8,128)(2,1)} %all-gather.9.cloned.1.call-done.all_ref, bf16[1024,192]{1,0:T(8,128)(2,1)} %get-tuple-element.213.context_ref), custom_call_target="tpu_custom_call" | custom-call | flops 1048576 | bytes 65536 | tf_op jit(solution)/shard_map/pallas_call | solution.py:681
  314.9 13.6 %all-to-all-done.2 = bf16[8,320,128]{2,1,0:T(8,128)(2,1)S(1)} async-done(((bf16[8,320,128]{2,1,0:T(8,128)(2,1)}), bf16[8,320,128]{2,1,0:T(8,128)(2,1)S(1)}, u32[]{:S(2)}, u32[]{:S(2)}) %all-to-all-start.2) | async-done | bytes 655392 | tf_op jit(solution)/shard_map/all_to_all | solution.py:826
  331.3 4.3 %all-to-all-start.3 = ((bf16[16,16,1664]{2,1,0:T(8,128)(2,1)}), bf16[16,16,1664]{2,1,0:T(8,128)(2,1)}, u32[]{:S(2)}, u32[]{:S(2)}) async-start(bf16[16,16,1664]{2,1,0:T(8,128)(2,1)} %fusion.1), calls=%async_computation.3 | async-start | bytes 1703936 | tf_op jit(solution)/shard_map/all_to_all | solution.py:849
  343.8 5.3 %all-to-all-done.3 = bf16[16,16,1664]{2,1,0:T(8,128)(2,1)} async-done(((bf16[16,16,1664]{2,1,0:T(8,128)(2,1)}), bf16[16,16,1664]{2,1,0:T(8,128)(2,1)}, u32[]{:S(2)}, u32[]{:S(2)}) %all-to-all-start.3) | async-done | bytes 852000 | tf_op jit(solution)/shard_map/all_to_all | solution.py:849
  354.6 3.9 collective-permute-done.28
  359.1 6.3 %collective-permute-done.29 = f32[16,128]{1,0:T(8,128)S(1)} collective-permute-done((f32[16,128]{1,0:T(8,128)S(1)}, f32[16,128]{1,0:T(8,128)S(1)}, u32[]{:S(2)}, u32[]{:S(2)}) %collective-permute-start.29) | collective-permute-done | bytes 8224 | tf_op jit(solution)/shard_map/ppermute | solution.py:118
  366.3 4.3 %all-to-all-start.4 = ((bf16[16,16,1664]{2,1,0:T(8,128)(2,1)}), bf16[16,16,1664]{2,1,0:T(8,128)(2,1)}, u32[]{:S(2)}, u32[]{:S(2)}) async-start(bf16[16,16,1664]{2,1,0:T(8,128)(2,1)} %broadcast_in_dim.13), calls=%async_computation.4 | async-start | bytes 1703936 | tf_op jit(solution)/shard_map/all_to_all | solution.py:865
  373.9 7.5 %all-to-all-done.4 = bf16[16,16,1664]{2,1,0:T(8,128)(2,1)} async-done(((bf16[16,16,1664]{2,1,0:T(8,128)(2,1)}), bf16[16,16,1664]{2,1,0:T(8,128)(2,1)}, u32[]{:S(2)}, u32[]{:S(2)}) %all-to-all-start.4) | async-done | bytes 852000 | tf_op jit(solution)/shard_map/all_to_all | solution.py:865
  381.4 5.7 %collective-permute-start.33 = (bf16[16,16,1664]{2,1,0:T(8,128)(2,1)}, bf16[16,16,1664]{2,1,0:T(8,128)(2,1)S(1)}, u32[]{:S(2)}, u32[]{:S(2)}) collective-permute-start(bf16[16,16,1664]{2,1,0:T(8,128)(2,1)} %all-to-all-done.4), channel_id=1, source_target_pairs={{0,128},{128,0},{1,129},{129,1},{2,130},{130,2},{3,131},{131,3},{4... | collective-permute-start | bytes 2555912 | tf_op jit(solution)/shard_map/ppermute | solution.py:128
  (204 shorter events, 125.9 us)
Async XLA Ops:
  7.2 63.4 %all-gather.11.cloned.1.call-start = ((), (), s32[]{:S(2)}) async-start(), calls=%async_computation.9 | async-start | bytes 4866048 | tf_op jit(solution)/shard_map/all_gather | solution.py:738
  10.6 131.6 %all-gather.7.cloned.1.call-start = ((), (), s32[]{:S(2)}) async-start(), calls=%async_computation.6 | async-start | bytes 10027008 | tf_op jit(solution)/shard_map/all_gather | solution.py:766
  26.8 22.6 %collective-permute-start.3 = (bf16[4,128,1664]{2,1,0:T(8,128)(2,1)}, bf16[4,128,1664]{2,1,0:T(8,128)(2,1)}, u32[]{:S(2)}, u32[]{:S(2)}) collective-permute-start(bf16[4,128,1664]{2,1,0:T(8,128)(2,1)} %pad_maximum_fusion.1.refs_1_), channel_id=1, source_target_pairs={{0,32},{8,40},{16,48},{24,56},{32,64},{40,72},{48,80},{56,88},{64,... | collective-permute-start | bytes 5111816 | tf_op jit(solution)/shard_map/ppermute | solution.py:65
  28.1 21.3 %collective-permute-start.4 = (bf16[4,128,1664]{2,1,0:T(8,128)(2,1)}, bf16[4,128,1664]{2,1,0:T(8,128)(2,1)}, u32[]{:S(2)}, u32[]{:S(2)}) collective-permute-start(bf16[4,128,1664]{2,1,0:T(8,128)(2,1)} %pad_maximum_fusion.1.refs_1_), channel_id=1, source_target_pairs={{0,96},{8,104},{16,112},{24,120},{32,0},{40,8},{48,16},{56,24},{64... | collective-permute-start | bytes 5111816 | tf_op jit(solution)/shard_map/ppermute | solution.py:65
  29.6 39.3 %collective-permute-start.5 = (bf16[4,128,1664]{2,1,0:T(8,128)(2,1)}, bf16[4,128,1664]{2,1,0:T(8,128)(2,1)}, u32[]{:S(2)}, u32[]{:S(2)}) collective-permute-start(bf16[4,128,1664]{2,1,0:T(8,128)(2,1)} %pad_maximum_fusion.1.refs_1_), channel_id=1, source_target_pairs={{0,64},{8,72},{16,80},{24,88},{32,96},{40,104},{48,112},{56,120},{... | collective-permute-start | bytes 5111816 | tf_op jit(solution)/shard_map/ppermute | solution.py:65
  76.1 20.8 %collective-permute-start.6 = (bf16[8,48,1536]{2,1,0:T(8,128)(2,1)}, bf16[8,48,1536]{2,1,0:T(8,128)(2,1)}, u32[]{:S(2)}, u32[]{:S(2)}) collective-permute-start(bf16[8,48,1536]{2,1,0:T(8,128)(2,1)} %get-tuple-element.244), channel_id=1, source_target_pairs={{0,8},{8,16},{16,24},{24,0},{32,40},{40,48},{48,56},{56,32},{64,72... | collective-permute-start | bytes 3538952 | tf_op jit(solution)/shard_map/ppermute | solution.py:65
  77.2 27.7 %collective-permute-start.7 = (bf16[8,48,1536]{2,1,0:T(8,128)(2,1)}, bf16[8,48,1536]{2,1,0:T(8,128)(2,1)}, u32[]{:S(2)}, u32[]{:S(2)}) collective-permute-start(bf16[8,48,1536]{2,1,0:T(8,128)(2,1)} %get-tuple-element.244), channel_id=1, source_target_pairs={{0,24},{8,0},{16,8},{24,16},{32,56},{40,32},{48,40},{56,48},{64,88... | collective-permute-start | bytes 3538952 | tf_op jit(solution)/shard_map/ppermute | solution.py:65
  78.8 28.5 %collective-permute-start.8 = (bf16[8,48,1536]{2,1,0:T(8,128)(2,1)}, bf16[8,48,1536]{2,1,0:T(8,128)(2,1)S(1)}, u32[]{:S(2)}, u32[]{:S(2)}) collective-permute-start(bf16[8,48,1536]{2,1,0:T(8,128)(2,1)} %get-tuple-element.244), channel_id=1, source_target_pairs={{0,16},{8,24},{16,0},{24,8},{32,48},{40,56},{48,32},{56,40},{64,80... | collective-permute-start | bytes 3538952 | tf_op jit(solution)/shard_map/ppermute | solution.py:65
  90.9 23.6 %all-to-all-start = ((bf16[8,192,128]{2,1,0:T(8,128)(2,1)}), bf16[8,192,128]{2,1,0:T(8,128)(2,1)S(1)}, u32[]{:S(2)}, u32[]{:S(2)}) async-start(bf16[8,192,128]{2,1,0:T(8,128)(2,1)} %get-tuple-element.132), calls=%async_computation | async-start | bytes 786432 | tf_op jit(solution)/shard_map/all_to_all | solution.py:770
  96.9 118.9 %all-gather.13.cloned.1.call-start = ((), (), s32[]{:S(2)}) async-start(), calls=%async_computation.10 | async-start | bytes 4423680 | tf_op jit(solution)/shard_map/all_gather | solution.py:777
  114.5 188.6 %all-gather.9.cloned.1.call-start = ((), (), s32[]{:S(2)}) async-start(), calls=%async_computation.7 | async-start | bytes 3538944 | tf_op jit(solution)/shard_map/all_gather | solution.py:827
  133.4 22.5 %collective-permute-start.12 = (bf16[4,128,1664]{2,1,0:T(8,128)(2,1)}, bf16[4,128,1664]{2,1,0:T(8,128)(2,1)}, u32[]{:S(2)}, u32[]{:S(2)}) collective-permute-start(bf16[4,128,1664]{2,1,0:T(8,128)(2,1)} %pad_maximum_fusion.2.refs_0_), channel_id=1, source_target_pairs={{0,32},{8,40},{16,48},{24,56},{32,64},{40,72},{48,80},{56,88},{64,... | collective-permute-start | bytes 5111816 | tf_op jit(solution)/shard_map/ppermute | solution.py:65
  134.8 21.7 %collective-permute-start.13 = (bf16[4,128,1664]{2,1,0:T(8,128)(2,1)}, bf16[4,128,1664]{2,1,0:T(8,128)(2,1)S(1)}, u32[]{:S(2)}, u32[]{:S(2)}) collective-permute-start(bf16[4,128,1664]{2,1,0:T(8,128)(2,1)} %pad_maximum_fusion.2.refs_0_), channel_id=1, source_target_pairs={{0,96},{8,104},{16,112},{24,120},{32,0},{40,8},{48,16},{56,24},{64... | collective-permute-start | bytes 5111816 | tf_op jit(solution)/shard_map/ppermute | solution.py:65
  156.4 24.0 %collective-permute-start.16 = (bf16[4,128,1664]{2,1,0:T(8,128)(2,1)}, bf16[4,128,1664]{2,1,0:T(8,128)(2,1)S(1)}, u32[]{:S(2)}, u32[]{:S(2)}) collective-permute-start(bf16[4,128,1664]{2,1,0:T(8,128)(2,1)} %pad_maximum_fusion.2.refs_0_), channel_id=1, source_target_pairs={{0,64},{8,72},{16,80},{24,88},{32,96},{40,104},{48,112},{56,120},{... | collective-permute-start | bytes 5111816 | tf_op jit(solution)/shard_map/ppermute | solution.py:65
  178.4 39.3 %collective-permute-start.14 = (bf16[4,128,1664]{2,1,0:T(8,128)(2,1)}, bf16[4,128,1664]{2,1,0:T(8,128)(2,1)}, u32[]{:S(2)}, u32[]{:S(2)}) collective-permute-start(bf16[4,128,1664]{2,1,0:T(8,128)(2,1)} %get-tuple-element.152), channel_id=1, source_target_pairs={{0,96},{8,104},{16,112},{24,120},{32,0},{40,8},{48,16},{56,24},{64... | collective-permute-start | bytes 5111816 | tf_op jit(solution)/shard_map/ppermute | solution.py:65
  180.3 40.9 %collective-permute-start.15 = (bf16[4,128,1664]{2,1,0:T(8,128)(2,1)}, bf16[4,128,1664]{2,1,0:T(8,128)(2,1)}, u32[]{:S(2)}, u32[]{:S(2)}) collective-permute-start(bf16[4,128,1664]{2,1,0:T(8,128)(2,1)} %get-tuple-element.153), channel_id=1, source_target_pairs={{0,32},{8,40},{16,48},{24,56},{32,64},{40,72},{48,80},{56,88},{64,... | collective-permute-start | bytes 5111816 | tf_op jit(solution)/shard_map/ppermute | solution.py:65
  193.7 27.5 %collective-permute-start.17 = (bf16[4,128,1664]{2,1,0:T(8,128)(2,1)}, bf16[4,128,1664]{2,1,0:T(8,128)(2,1)}, u32[]{:S(2)}, u32[]{:S(2)}) collective-permute-start(bf16[4,128,1664]{2,1,0:T(8,128)(2,1)} %get-tuple-element.162), channel_id=1, source_target_pairs={{0,64},{8,72},{16,80},{24,88},{32,96},{40,104},{48,112},{56,120},{... | collective-permute-start | bytes 5111816 | tf_op jit(solution)/shard_map/ppermute | solution.py:65
  221.2 18.5 %collective-permute-start.19 = (bf16[6,768,512]{2,1,0:T(8,128)(2,1)}, bf16[6,768,512]{2,1,0:T(8,128)(2,1)S(1)}, u32[]{:S(2)}, u32[]{:S(2)}) collective-permute-start(bf16[6,768,512]{2,1,0:T(8,128)(2,1)} %shard_map.253), channel_id=1, source_target_pairs={{0,128},{128,0},{1,129},{129,1},{2,130},{130,2},{3,131},{131,3},{4... | collective-permute-start | bytes 14155784 | tf_op jit(solution)/shard_map/ppermute | solution.py:128
  232.4 13.1 %collective-permute-start.20 = (bf16[128,1664]{1,0:T(8,128)(2,1)S(1)}, bf16[128,1664]{1,0:T(8,128)(2,1)S(1)}, u32[]{:S(2)}, u32[]{:S(2)}) collective-permute-start(bf16[128,1664]{1,0:T(8,128)(2,1)S(1)} %get-tuple-element.199), channel_id=1, source_target_pairs={{0,8},{8,16},{16,24},{24,0},{32,40},{40,48},{48,56},{56,32},{64,72... | collective-permute-start | bytes 1277960 | tf_op jit(solution)/shard_map/ppermute | solution.py:65
  253.0 17.2 %all-to-all-start.1 = ((bf16[8,192,128]{2,1,0:T(8,128)(2,1)}), bf16[8,192,128]{2,1,0:T(8,128)(2,1)S(1)}, u32[]{:S(2)}, u32[]{:S(2)}) async-start(bf16[8,192,128]{2,1,0:T(8,128)(2,1)} %bitcast.25), calls=%async_computation.1 | async-start | bytes 786432 | tf_op jit(solution)/shard_map/all_to_all | solution.py:820
  256.4 125.0 %reduce-scatter.2.cloned.1.call-start = ((), (), s32[]{:S(2)}) async-start(), calls=%async_computation.8 | async-start | bytes 5308416 | tf_op jit(solution)/shard_map/reduce_scatter | solution.py:824
  270.9 68.6 %collective-permute-start.26 = (bf16[8,160,1536]{2,1,0:T(8,128)(2,1)}, bf16[8,160,1536]{2,1,0:T(8,128)(2,1)}, u32[]{:S(2)}, u32[]{:S(2)}) collective-permute-start(bf16[8,160,1536]{2,1,0:T(8,128)(2,1)} %bitcast.100), channel_id=1, source_target_pairs={{0,128},{128,0},{1,129},{129,1},{2,130},{130,2},{3,131},{131,3},{4... | collective-permute-start | bytes 11796488 | tf_op jit(solution)/shard_map/ppermute | solution.py:128
  277.0 34.8 %collective-permute-start.23 = (bf16[4,128,1536]{2,1,0:T(8,128)(2,1)}, bf16[4,128,1536]{2,1,0:T(8,128)(2,1)}, u32[]{:S(2)}, u32[]{:S(2)}) collective-permute-start(bf16[4,128,1536]{2,1,0:T(8,128)(2,1)} %get-tuple-element.217), channel_id=1, source_target_pairs={{0,96},{8,104},{16,112},{24,120},{32,0},{40,8},{48,16},{56,24},{64... | collective-permute-start | bytes 4718600 | tf_op jit(solution)/shard_map/ppermute | solution.py:65
  277.0 37.9 %collective-permute-start.24 = (bf16[4,128,1536]{2,1,0:T(8,128)(2,1)}, bf16[4,128,1536]{2,1,0:T(8,128)(2,1)}, u32[]{:S(2)}, u32[]{:S(2)}) collective-permute-start(bf16[4,128,1536]{2,1,0:T(8,128)(2,1)} %get-tuple-element.218), channel_id=1, source_target_pairs={{0,32},{8,40},{16,48},{24,56},{32,64},{40,72},{48,80},{56,88},{64,... | collective-permute-start | bytes 4718600 | tf_op jit(solution)/shard_map/ppermute | solution.py:65
  278.4 36.5 %collective-permute-start.25 = (bf16[4,128,1536]{2,1,0:T(8,128)(2,1)}, bf16[4,128,1536]{2,1,0:T(8,128)(2,1)}, u32[]{:S(2)}, u32[]{:S(2)}) collective-permute-start(bf16[4,128,1536]{2,1,0:T(8,128)(2,1)} %get-tuple-element.219), channel_id=1, source_target_pairs={{0,64},{8,72},{16,80},{24,88},{32,96},{40,104},{48,112},{56,120},{... | collective-permute-start | bytes 4718600 | tf_op jit(solution)/shard_map/ppermute | solution.py:65
  299.4 29.1 %all-to-all-start.2 = ((bf16[8,320,128]{2,1,0:T(8,128)(2,1)}), bf16[8,320,128]{2,1,0:T(8,128)(2,1)S(1)}, u32[]{:S(2)}, u32[]{:S(2)}) async-start(bf16[8,320,128]{2,1,0:T(8,128)(2,1)} %get-tuple-element.215), calls=%async_computation.2 | async-start | bytes 1310720 | tf_op jit(solution)/shard_map/all_to_all | solution.py:826
  310.0 18.5 %collective-permute-start.22 = (bf16[16,16,1664]{2,1,0:T(8,128)(2,1)}, bf16[16,16,1664]{2,1,0:T(8,128)(2,1)}, u32[]{:S(2)}, u32[]{:S(2)}) collective-permute-start(bf16[16,16,1664]{2,1,0:T(8,128)(2,1)} %fusion.5), channel_id=1, source_target_pairs={{0,128},{128,0},{1,129},{129,1},{2,130},{130,2},{3,131},{131,3},{4... | collective-permute-start | bytes 2555912 | tf_op jit(solution)/shard_map/ppermute | solution.py:128
  331.3 17.8 %all-to-all-start.3 = ((bf16[16,16,1664]{2,1,0:T(8,128)(2,1)}), bf16[16,16,1664]{2,1,0:T(8,128)(2,1)}, u32[]{:S(2)}, u32[]{:S(2)}) async-start(bf16[16,16,1664]{2,1,0:T(8,128)(2,1)} %fusion.1), calls=%async_computation.3 | async-start | bytes 1703936 | tf_op jit(solution)/shard_map/all_to_all | solution.py:849
  350.5 22.0 %collective-permute-start.32 = (bf16[128,1536]{1,0:T(8,128)(2,1)}, bf16[128,1536]{1,0:T(8,128)(2,1)}, u32[]{:S(2)}, u32[]{:S(2)}) collective-permute-start(bf16[128,1536]{1,0:T(8,128)(2,1)} %copy-done.13), channel_id=1, source_target_pairs={{0,16},{8,24},{16,0},{24,8},{32,48},{40,56},{48,32},{56,40},{64,80... | collective-permute-start | bytes 1179656 | tf_op jit(solution)/shard_map/ppermute | solution.py:65
  351.7 20.8 %collective-permute-start.31 = (bf16[128,1536]{1,0:T(8,128)(2,1)}, bf16[128,1536]{1,0:T(8,128)(2,1)}, u32[]{:S(2)}, u32[]{:S(2)}) collective-permute-start(bf16[128,1536]{1,0:T(8,128)(2,1)} %copy-done.12), channel_id=1, source_target_pairs={{0,8},{8,16},{16,24},{24,0},{32,40},{40,48},{48,56},{56,32},{64,72... | collective-permute-start | bytes 1179656 | tf_op jit(solution)/shard_map/ppermute | solution.py:65
  352.4 20.1 %collective-permute-start.30 = (bf16[128,1536]{1,0:T(8,128)(2,1)S(1)}, bf16[128,1536]{1,0:T(8,128)(2,1)}, u32[]{:S(2)}, u32[]{:S(2)}) collective-permute-start(bf16[128,1536]{1,0:T(8,128)(2,1)S(1)} %get-tuple-element.234), channel_id=1, source_target_pairs={{0,24},{8,0},{16,8},{24,16},{32,56},{40,32},{48,40},{56,48},{64,88... | collective-permute-start | bytes 1179656 | tf_op jit(solution)/shard_map/ppermute | solution.py:65
  366.3 15.1 %all-to-all-start.4 = ((bf16[16,16,1664]{2,1,0:T(8,128)(2,1)}), bf16[16,16,1664]{2,1,0:T(8,128)(2,1)}, u32[]{:S(2)}, u32[]{:S(2)}) async-start(bf16[16,16,1664]{2,1,0:T(8,128)(2,1)} %broadcast_in_dim.13), calls=%async_computation.4 | async-start | bytes 1703936 | tf_op jit(solution)/shard_map/all_to_all | solution.py:865
  (45 other events, 334.5 us)
Sparse Core Ops, SparseCore 0:
  10.7 59.8 all-gather.10
  73.0 69.1 all-gather.6
  144.0 50.4 all-gather.12
  253.1 45.3 all-gather.8
  300.9 65.7 reduce-scatter.1
